TPU v7x, 32 devices: a whole 2x2x4 slice. The times are simulated.
32 devices in a mesh: row: 8 (over y, x, core), col: 4 (over z).
Axes of the slice: x: 2, y: 2, z: 4, core: 2. Of those that a mesh axis runs over, the one named last changes fastest.
Arguments:
- features: bfloat16 [4096, 2048], P(('row', 'col')), may hold values from -20 to 20
- weight_one: bfloat16 [2048, 2048], replicated, may hold values from -0.25 to 0.25
- bias_one: float32 [2048], replicated, may hold values from -3 to 3
- weight_two: bfloat16 [2048, 2048], replicated, may hold values from -0.25 to 0.25
- bias_two: float32 [2048], replicated, may hold values from -3 to 3
- cotangent: bfloat16 [4096, 2048], P(('row', 'col')), may hold values from -6 to 6
- neighbours: int32 [4096, 16], P('row'), may hold values from -1 to 4095, as said below
- valid_mask: int32 [4096], P(('row', 'col')), may hold values from 0 to 1
Outputs:
- act: bfloat16 [4096, 2048], P(('row', 'col'))
- grad_input: bfloat16 [4096, 2048], P(('row', 'col'))
- grad_weight_one: float32 [2048, 2048], P(('row', 'col'))
- grad_bias_one: float32 [2048], P(('row', 'col'))
- grad_weight_two: float32 [2048, 2048], P(('row', 'col'))
- grad_bias_two: float32 [2048], P(('row', 'col'))
- rms_stats: float32 [2, 3], replicated
Inputs may be any that keep to these rules, and one draw needn't show every extreme that they name: `neighbours`: an entry is a node that row i aggregates, or -1 for an empty slot. No entry names a node whose valid_mask is 0, and the rows of such nodes hold only -1.
All inputs are finite; a program needn't handle non-finite values.
Results may differ from a plain program's by a relative error of at most 0.012.
The roundings to bfloat16 on the way count: a program that leaves them out, or rounds other values in their place, can miss the bound.
Values may be sent and summed in bfloat16 or wider, within the bound.
No kernel may reach another device: no remote copies, remote signals or barrier semaphores. Data moves between devices by JAX's collectives and lax.ppermute only.
A program may use at most 192 MiB of HBM per device.

v0:
```python
import functools

import jax
import jax.numpy as jnp
from jax import lax
from jax.experimental import pallas as pl
from jax.experimental.pallas import tpu as pltpu
from jax.sharding import Mesh
from jax.sharding import PartitionSpec as P

BF16, F32 = jnp.bfloat16, jnp.float32
LANES = 128
MXU = 256
MIB = 1 << 20
NT = (((1,), (1,)), ((), ()))
GELU_C, GELU_A = 0.7978845608, 0.044715


def gelu_value(value):
    return jax.nn.gelu(value, approximate=True)


def source_parts(lists, per_dev, col_devs):
    live = lists >= 0
    safe = jnp.maximum(lists, 0)
    block = safe // per_dev
    return (live, block // col_devs, block % col_devs, safe % per_dev)


def block_tile(lists, usable, local_index, span):
    columns = jnp.arange(span, dtype=jnp.int32)[None, :]
    marked = jnp.where(usable, local_index, -1)
    total = jnp.zeros((lists.shape[0], span), jnp.float32)
    for slot in range(lists.shape[1]):
        total = total + (marked[:, slot : slot + 1] == columns).astype(jnp.float32)
    return total.astype(jnp.bfloat16)


def reduce_weights(grad_weight, grad_bias):
    return (
        lax.psum_scatter(grad_weight, ("row", "col"), scatter_dimension=0, tiled=True),
        lax.psum_scatter(grad_bias, ("row", "col"), scatter_dimension=0, tiled=True),
    )


def general(features, weight_one, bias_one, weight_two, bias_two, cotangent, neighbours, valid_mask):
    per_dev, width = features.shape
    row_devs = lax.axis_size("row")
    col_devs = lax.axis_size("col")
    col_pos = lax.axis_index("col")
    own_lists = lax.dynamic_slice_in_dim(neighbours, col_pos * per_dev, per_dev, 0)
    inverse = 1.0 / (jnp.sum(own_lists >= 0, axis=1).astype(jnp.float32) + 1.0)
    scaling = inverse[:, None]
    validity = valid_mask.astype(jnp.float32)[:, None]
    live, src_row, src_col, offset = source_parts(neighbours, per_dev, col_devs)
    front_tile = block_tile(
        neighbours, live & (src_col == col_pos), src_row * per_dev + offset, row_devs * per_dev
    )

    def forward_layer(inputs, weight, bias):
        gathered = lax.all_gather(inputs, "row", axis=0, tiled=True)
        partial_value = jnp.dot(front_tile, gathered, preferred_element_type=jnp.float32)
        summed = lax.psum_scatter(partial_value, "col", scatter_dimension=0, tiled=True)
        aggregate = ((summed + 2.0 * inputs.astype(jnp.float32)) * scaling).astype(jnp.bfloat16)
        preact = jnp.dot(aggregate, weight, preferred_element_type=jnp.float32) + bias
        return (aggregate, preact, validity * gelu_value(preact))

    agg_one, pre_one, out_one = forward_layer(features, weight_one, bias_one)
    hidden = out_one.astype(jnp.bfloat16)
    agg_two, pre_two, out_two = forward_layer(hidden, weight_two, bias_two)

    def squares(value):
        return jnp.sum(validity * jnp.square(value.astype(jnp.float32)))

    local_squares = jnp.stack(
        [
            squares(features),
            squares(agg_one),
            squares(out_one),
            squares(hidden),
            squares(agg_two),
            squares(out_two),
        ]
    ).reshape(2, 3)
    total_squares, total_valid = lax.psum((local_squares, jnp.sum(validity)), ("row", "col"))
    rms_stats = jnp.sqrt(total_squares / (total_valid * width) + 1e-06)

    def backward_layer(upstream, aggregate, preact, weight):
        grad_act = validity * upstream
        grad_pre = jax.vjp(gelu_value, preact)[1](grad_act)[0].astype(jnp.bfloat16)
        grad_weight = lax.dot_general(
            aggregate, grad_pre, (((0,), (0,)), ((), ())), preferred_element_type=jnp.float32
        )
        grad_bias = jnp.sum(grad_pre.astype(jnp.float32), axis=0)
        grad_low = lax.dot_general(
            grad_pre, weight, (((1,), (1,)), ((), ())), preferred_element_type=jnp.float32
        ).astype(jnp.bfloat16)
        grad_agg = lax.optimization_barrier(grad_low).astype(jnp.float32)
        grad_sum = (grad_agg * scaling).astype(jnp.bfloat16)
        grad_all = lax.all_gather(grad_sum, "col", axis=0, tiled=True)
        from_lists = lax.psum_scatter(
            lax.dot_general(
                front_tile, grad_all, (((0,), (0,)), ((), ())), preferred_element_type=jnp.float32
            ),
            "row",
            scatter_dimension=0,
            tiled=True,
        )
        return (from_lists + 2.0 * grad_agg * scaling, grad_weight, grad_bias)

    grad_hidden, weight_grad_two, bias_grad_two = backward_layer(
        cotangent.astype(jnp.float32), agg_two, pre_two, weight_two
    )
    weight_grad_two, bias_grad_two = reduce_weights(weight_grad_two, bias_grad_two)
    grad_start, weight_grad_one, bias_grad_one = backward_layer(
        grad_hidden, agg_one, pre_one, weight_one
    )
    weight_grad_one, bias_grad_one = reduce_weights(weight_grad_one, bias_grad_one)
    return (
        out_two.astype(jnp.bfloat16),
        grad_start.astype(jnp.bfloat16),
        weight_grad_one,
        bias_grad_one,
        weight_grad_two,
        bias_grad_two,
        rms_stats,
    )


IN_VMEM = pl.BlockSpec(memory_space=pltpu.VMEM)
IN_SMEM = pl.BlockSpec(memory_space=pltpu.SMEM)
IN_ANY = pl.BlockSpec(memory_space=pl.ANY)
COUNT = jnp.float8_e4m3fn
PARAMS = pltpu.CompilerParams(vmem_limit_bytes=48 * MIB)


def cost(flops, read, transcendentals=0):
    return pl.CostEstimate(flops=flops, bytes_accessed=read, transcendentals=transcendentals)


def lanes(at, size=LANES):
    return slice(at * size, (at + 1) * size)


def fetch(source, target, semaphore):
    copy = pltpu.make_async_copy(source, target, semaphore)
    copy.start()
    return copy


def stream(source, blocks, target, semaphores):
    copies = [fetch(source.at[block], target.at[block], semaphores.at[i]) for i, block in enumerate(blocks)]

    def arrivals():
        for block, copy in zip(blocks, copies, strict=True):
            copy.wait()
            yield target[block]

    return arrivals()


def buffer(shape, blocks, dtype=BF16):
    return [pltpu.VMEM(shape, dtype), pltpu.SemaphoreType.DMA((blocks,))]


def like(value):
    return [pltpu.VMEM(value.shape, value.dtype), pltpu.SemaphoreType.DMA]


class Results:
    def __init__(self, semaphores):
        self.semaphores, self.copies = semaphores, []

    def send(self, source, target):
        self.copies.append(fetch(source, target, self.semaphores.at[len(self.copies)]))

    def wait(self):
        for copy in self.copies:
            copy.wait()


def column_blocks(size, step):
    return [(slice(None), slice(at, at + step)) for at in range(0, size, step)]


def row_blocks(size, step):
    return [(slice(at, at + step), slice(None)) for at in range(0, size, step)]


def tile_kernel(turn, nodes, cols, place_ref, lists_ref, tile_ref):
    masks, lines, width = lists_ref.shape
    groups = 8
    rows = LANES // groups
    chip_row, core = place_ref[0] // 2, place_ref[0] % 2
    step = pl.program_id(0)
    per_chip = lines // groups
    mask = chip_row ^ (step // per_chip)
    lists = lists_ref[mask, pl.ds(pl.multiple_of(step % per_chip * groups, groups), groups), :]
    node_bits, col_bits = nodes.bit_length() - 1, cols.bit_length() - 1
    owner_row = lists >> (node_bits + col_bits)
    within = lists & (nodes * cols - 1)
    place = ((owner_row >> 1) << (node_bits + col_bits)) + within
    live = lists >= 0
    if turn:
        half = masks * cols * nodes
        place = jnp.where((owner_row & 1) == core, place, place + half)
    else:
        live &= (owner_row & 1) == core
    line = lax.broadcasted_iota(jnp.int32, lists.shape, 1) // rows
    highs = jnp.where(live, (place // MXU) * rows + line, -1)
    lows = place % MXU
    blocks = (tile_ref.shape[0] if turn else tile_ref.shape[1]) // MXU
    high_place = lax.broadcasted_iota(jnp.int32, (blocks * rows, width), 0)
    low_place = lax.broadcasted_iota(jnp.int32, (MXU, width), 0)
    pieces = []
    for group in range(groups):
        high = (high_place == highs[group : group + 1, :]).astype(F32).astype(BF16)
        low = (low_place == lows[group : group + 1, :]).astype(F32).astype(BF16)
        counts = lax.dot_general(high, low, NT, preferred_element_type=F32)
        pieces.append(counts.astype(BF16))
    for block in range(blocks):
        column = jnp.concatenate([piece[block * rows : (block + 1) * rows] for piece in pieces], axis=0)
        if turn:
            for side in range(2):
                turned = column[:, lanes(side)].T
                tile_ref[lanes(2 * block + side), :] = turned.astype(COUNT)
        else:
            tile_ref[:, lanes(block, MXU)] = column.astype(COUNT)


def count_tile(at, lists, nodes, cols, turn):
    masks, lines, width = lists.shape
    rows = masks * lines * 16
    half = masks * cols * nodes
    shape = (2 * half, rows) if turn else (rows, half)
    block = (2 * half, LANES) if turn else (LANES, half)
    return pl.pallas_call(
        functools.partial(tile_kernel, turn, nodes, cols),
        grid=(rows // LANES,),
        in_specs=[IN_SMEM, pl.BlockSpec(lists.shape, lambda i: (0, 0, 0))],
        out_specs=pl.BlockSpec(block, (lambda i: (0, i)) if turn else (lambda i: (i, 0))),
        out_shape=jax.ShapeDtypeStruct(shape, COUNT),
        compiler_params=PARAMS,
        cost_estimate=cost(4 * rows * shape[0 if turn else 1] * 2 * MXU, rows * half),
    )(at, lists)


def adjacency_kernel(forward, tiles, own_ref, other_ref, *refs):
    tile_refs, refs = refs[:tiles], refs[-10 - tiles :]
    out_ref, left_ref, total_ref, own, own_sem, other, other_sem = refs[:7]
    buffers, (semaphores, out, out_sems) = refs[7 : 7 + tiles], refs[7 + tiles :]
    chips, width = own_ref.shape[0], LANES
    half = chips * width
    copies = [fetch(own_ref, own, own_sem), fetch(other_ref, other, other_sem)]
    chunks, arrivals = [], []
    for ref, target in zip(tile_refs, buffers, strict=True):
        for at in range(0, ref.shape[0], half):
            here = slice(at, at + half)
            arrivals.append(fetch(ref.at[here], target.at[here], semaphores.at[len(chunks)]))
            chunks.append(target.at[here])
    for copy in copies:
        copy.wait()
    for at in range(chips):
        left_ref[:width, lanes(at)] = own[at].T if forward else own[at]
        left_ref[:width, lanes(chips + at)] = other[at].T if forward else other[at]
    if forward:
        left_ref[width:, :] = jnp.ones((left_ref.shape[0] - width, left_ref.shape[1]), BF16)
    for block, (copy, counts) in enumerate(zip(arrivals, chunks, strict=True)):
        copy.wait()
        part = jnp.dot(left_ref[:, lanes(block, half)], counts[...].astype(BF16), preferred_element_type=F32)
        if block == 0:
            total_ref[...] = part
        else:
            total_ref[...] += part
    results = Results(out_sems)
    group = chips // out_sems.shape[0]
    for at in range(chips):
        here = lanes(at)
        if forward:
            inverse = 1.0 / (total_ref[width : width + 1, here] + 1.0)
            value = (total_ref[:width, here] + 2.0 * left_ref[:width, here].astype(F32)) * inverse
            out[at] = value.astype(BF16).T
        else:
            out[at] = total_ref[:, here].astype(BF16)
        if (at + 1) % group == 0:
            done = slice(at + 1 - group, at + 1)
            results.send(out.at[done], out_ref.at[done])
    results.wait()


def apply_adjacency(tiles, own, other, forward, *after):
    sources, half = sum(tile.shape[0] for tile in tiles), tiles[0].shape[1]
    rows = LANES + (16 if forward else 0)
    scratch = [pltpu.VMEM((rows, sources), BF16), pltpu.VMEM((rows, half), F32)] + like(own) + like(other)
    scratch += [pltpu.VMEM(tile.shape, COUNT) for tile in tiles] + [pltpu.SemaphoreType.DMA((sources // half,))]
    return pl.pallas_call(
        functools.partial(adjacency_kernel, forward, len(tiles)),
        in_specs=[IN_ANY] * (2 + len(tiles) + len(after)),
        out_specs=IN_ANY,
        out_shape=jax.ShapeDtypeStruct(own.shape, BF16),
        scratch_shapes=scratch + buffer(own.shape, 4),
        compiler_params=PARAMS,
        cost_estimate=cost(2 * half * sources * LANES, half * sources),
    )(own, other, *tiles, *after)


def gelu_parts(pre, valid):
    square = pre * pre
    bend = jnp.tanh(GELU_C * (pre + GELU_A * (square * pre)))
    inner = GELU_C * (1.0 + 3.0 * GELU_A * square)
    slope = 0.5 * (1.0 + bend) + 0.5 * pre * (1.0 - bend * bend) * inner
    return valid * (0.5 * pre * (1.0 + bend)), valid * slope


def lane_squares(value, valid):
    value = value.astype(F32)
    value = jnp.sum(valid * (value * value), axis=0, keepdims=True)
    return sum(value[:, lanes(i)] for i in range(value.shape[1] // LANES))


def send_pieces(at_ref, agg_blocks, pieces, piece_refs, results):
    chip_row = at_ref[0] // 2
    blocks = agg_blocks.shape[0] // len(piece_refs)
    for mask, ref in enumerate(piece_refs):
        for part in range(blocks):
            pieces[mask, :, lanes(part)] = agg_blocks[(chip_row ^ mask) * blocks + part]
        results.send(pieces.at[mask], ref)


def first_kernel(at_ref, agg_ref, weight_ref, bias_ref, valid_ref, input_ref, *refs):
    out_ref, slope_ref, stat_ref = refs[-17:-14]
    piece_refs = refs[-14:-10]
    agg_blocks, agg_sem, inputs, input_sem, weight_buffer, semaphores = refs[-10:-4]
    out, slopes, pieces, out_sems = refs[-4:]
    chips, nodes, width = agg_ref.shape
    full = weight_ref.shape[1]
    step = full // semaphores.shape[0]
    copies = [fetch(agg_ref, agg_blocks, agg_sem)]
    weights = stream(weight_ref, column_blocks(full, step), weight_buffer, semaphores)
    copies.append(fetch(input_ref, inputs, input_sem))
    results = Results(out_sems)
    valid = valid_ref[...]
    copies[0].wait()
    agg = jnp.concatenate([agg_blocks[i] for i in range(chips)], axis=1)
    send_pieces(at_ref, agg_blocks, pieces, piece_refs, results)
    none = jnp.zeros((1, LANES), F32)
    of_agg, of_input, of_out, of_low = lane_squares(agg, valid), none, none, none
    for block, weight in enumerate(weights):
        here = lanes(block, step)
        pre = jnp.dot(agg, weight, preferred_element_type=F32) + bias_ref[:, here]
        value, slopes[:, here] = gelu_parts(pre, valid)
        low = value.astype(BF16)
        of_out += lane_squares(value, valid)
        of_low += lane_squares(low, valid)
        if block == 0:
            copies[1].wait()
        of_input += lane_squares(inputs[:, here], valid)
        blocks = lanes(block, step // LANES)
        for part in range(step // LANES):
            out[blocks.start + part] = low[:, lanes(part)]
        results.send(out.at[blocks], out_ref.at[blocks])
        results.send(slopes.at[:, here], slope_ref.at[:, here])
    count = jnp.sum(jnp.broadcast_to(valid, (nodes, LANES)), axis=0, keepdims=True) * (1.0 / LANES)
    stat_ref[...] = jnp.concatenate([of_input, of_agg, of_out, of_low, count, none, none, none], axis=0)
    results.wait()


def piece_shapes(agg, chip_rows):
    chips, nodes, width = agg.shape
    return [jax.ShapeDtypeStruct((nodes, chips * width // chip_rows), BF16)] * chip_rows


def first_layer(at, agg, weight, bias, valid, inputs, chip_rows, *after):
    chips, nodes, width = agg.shape
    full = weight.shape[1]
    pieces = piece_shapes(agg, chip_rows)
    steps = 2
    return pl.pallas_call(
        first_kernel,
        in_specs=[IN_SMEM, IN_ANY, IN_ANY, IN_VMEM, IN_VMEM, IN_ANY] + [IN_ANY] * len(after),
        out_specs=[IN_ANY, IN_ANY, IN_VMEM] + [IN_ANY] * chip_rows,
        out_shape=[
            jax.ShapeDtypeStruct(agg.shape, BF16),
            jax.ShapeDtypeStruct((nodes, full), F32),
            jax.ShapeDtypeStruct((8, LANES), F32),
        ]
        + pieces,
        scratch_shapes=like(agg)
        + like(inputs)
        + buffer(weight.shape, steps)
        + [
            pltpu.VMEM(agg.shape, BF16),
            pltpu.VMEM((nodes, full), F32),
            pltpu.VMEM((chip_rows,) + pieces[0].shape, BF16),
            pltpu.SemaphoreType.DMA((chip_rows + 2 * steps,)),
        ],
        compiler_params=PARAMS,
        cost_estimate=cost(2 * nodes * full * full, 2 * full * full, nodes * full),
    )(at, agg, weight, bias, valid, inputs, *after)


def gradient_blocks(weight, blocks, turned, inverse, outs, refs, results):
    low = jnp.dot(weight, turned[...], preferred_element_type=F32).astype(BF16)
    sums = (low.astype(F32) * inverse).astype(BF16)
    for value, out, ref in zip((sums, low), outs, refs, strict=True):
        for part in range(weight.shape[0] // LANES):
            out[blocks.start + part] = value[lanes(part)]
        results.send(out.at[blocks], ref.at[blocks])


def second_kernel(
    at_ref, agg_ref, weight_ref, bias_ref, valid_ref, cotangent_ref, inverse_ref, stat_ref, *refs
):
    act_ref, pre_ref, sums_ref, grad_agg_ref = refs[-21:-17]
    piece_refs = refs[-17:-13]
    agg_blocks, agg_sem, cotangent, cotangent_sem, weight_buffer, semaphores = refs[-13:-7]
    act, pres, turned, sums, grad_agg, pieces, out_sems = refs[-7:]
    chips, nodes, width = agg_ref.shape
    full = weight_ref.shape[1]
    step = full // semaphores.shape[0]
    copies = [fetch(agg_ref, agg_blocks, agg_sem)]
    weights = stream(weight_ref, column_blocks(full, step), weight_buffer, semaphores)
    copies.append(fetch(cotangent_ref, cotangent, cotangent_sem))
    results = Results(out_sems)
    valid, inverse = valid_ref[...], inverse_ref[...]
    copies[0].wait()
    agg = jnp.concatenate([agg_blocks[i] for i in range(chips)], axis=1)
    send_pieces(at_ref, agg_blocks, pieces, piece_refs, results)
    of_agg, of_out = lane_squares(agg, valid), jnp.zeros((1, LANES), F32)
    for block, weight in enumerate(weights):
        here = lanes(block, step)
        pre = jnp.dot(agg, weight, preferred_element_type=F32) + bias_ref[:, here]
        value, slope = gelu_parts(pre, valid)
        of_out += lane_squares(value, valid)
        act[:, here] = value.astype(BF16)
        results.send(act.at[:, here], act_ref.at[:, here])
        if block == 0:
            copies[1].wait()
        grad_pre = (cotangent[:, here].astype(F32) * slope).astype(BF16)
        pres[:, here] = grad_pre
        for part in range(step // LANES):
            turned[block * step + part * LANES : block * step + (part + 1) * LANES, :] = grad_pre[:, lanes(part)].T
    stat = stat_ref[...]
    rows = [stat[:4], of_agg, of_out, stat[4:5], jnp.zeros((1, LANES), F32)]
    total = jnp.sum(jnp.concatenate(rows, axis=0), axis=1, keepdims=True)
    high = total.astype(BF16).astype(F32)
    both = jnp.concatenate([high, total - high], axis=0)
    pres[:16, full:] = jnp.broadcast_to(both, (16, LANES)).astype(BF16)
    pres[16:, full:] = jnp.zeros((nodes - 16, LANES), BF16)
    results.send(pres, pre_ref)
    step = full // 4
    for block in range(4):
        gradient_blocks(
            weight_buffer[lanes(block, step), :], lanes(block, step // LANES), turned, inverse,
            (sums, grad_agg), (sums_ref, grad_agg_ref), results,
        )
    results.wait()


def second_layer(at, agg, weight, bias, valid, cotangent, inverse, stats, chip_rows, *after):
    chips, nodes, width = agg.shape
    full = weight.shape[1]
    blocks = jax.ShapeDtypeStruct((chips, width, nodes), BF16)
    pieces = piece_shapes(agg, chip_rows)
    steps = 2
    return pl.pallas_call(
        second_kernel,
        in_specs=[IN_SMEM, IN_ANY, IN_ANY, IN_VMEM, IN_VMEM, IN_ANY, IN_VMEM, IN_VMEM] + [IN_ANY] * len(after),
        out_specs=[IN_ANY] * (4 + chip_rows),
        out_shape=[
            jax.ShapeDtypeStruct((nodes, full), BF16),
            jax.ShapeDtypeStruct((nodes, full + LANES), BF16),
            blocks,
            blocks,
        ]
        + pieces,
        scratch_shapes=like(agg)
        + like(cotangent)
        + buffer(weight.shape, steps)
        + [
            pltpu.VMEM((nodes, full), BF16),
            pltpu.VMEM((nodes, full + LANES), BF16),
            pltpu.VMEM((full, nodes), BF16),
            pltpu.VMEM(blocks.shape, BF16),
            pltpu.VMEM(blocks.shape, BF16),
            pltpu.VMEM((chip_rows,) + pieces[0].shape, BF16),
            pltpu.SemaphoreType.DMA((chip_rows + steps + 1 + 8,)),
        ],
        compiler_params=PARAMS,
        cost_estimate=cost(4 * nodes * full * full, 2 * full * full, nodes * full),
    )(at, agg, weight, bias, valid, cotangent, inverse, stats, *after)


def back_kernel(slope_ref, weight_ref, inverse_ref, up_ref, extra_ref, *refs):
    pre_ref, sums_ref, agg_ref, slope, slope_sem, up, up_sem, extra, extra_sem = refs[-16:-7]
    weight_buffer, semaphores, pres, turned, sums, grad_agg, out_sems = refs[-7:]
    nodes, full = slope_ref.shape
    step = full // semaphores.shape[0]
    copies = [fetch(up_ref, up, up_sem), fetch(extra_ref, extra, extra_sem), fetch(slope_ref, slope, slope_sem)]
    weights = stream(weight_ref, row_blocks(full, step), weight_buffer, semaphores)
    results = Results(out_sems)
    inverse = inverse_ref[...]
    for copy in copies:
        copy.wait()
    for at in range(up_ref.shape[0]):
        value = up[at].astype(F32) + 2.0 * extra[at].astype(F32) * inverse
        grad_pre = (value.T * slope[:, lanes(at)]).astype(BF16)
        pres[:, lanes(at)] = grad_pre
        turned[lanes(at), :] = grad_pre.T
    pres[:, full:] = jnp.zeros((nodes, LANES), BF16)
    results.send(pres, pre_ref)
    for block, weight in enumerate(weights):
        gradient_blocks(
            weight, lanes(block, step // LANES), turned, inverse, (sums, grad_agg), (sums_ref, agg_ref), results
        )
    results.wait()


def first_layer_back(slope, weight, inverse, upstream, extra, *after):
    nodes, full = slope.shape
    blocks = jax.ShapeDtypeStruct(upstream.shape, BF16)
    steps = 1
    return pl.pallas_call(
        back_kernel,
        in_specs=[IN_ANY, IN_ANY, IN_VMEM, IN_ANY, IN_ANY] + [IN_ANY] * len(after),
        out_specs=[IN_ANY] * 3,
        out_shape=[jax.ShapeDtypeStruct((nodes, full + LANES), BF16), blocks, blocks],
        scratch_shapes=like(slope)
        + like(upstream)
        + like(extra)
        + buffer(weight.shape, steps)
        + [
            pltpu.VMEM((nodes, full + LANES), BF16),
            pltpu.VMEM((full, nodes), BF16),
            pltpu.VMEM(blocks.shape, BF16),
            pltpu.VMEM(blocks.shape, BF16),
            pltpu.SemaphoreType.DMA((1 + 2 * steps,)),
        ],
        compiler_params=PARAMS,
        cost_estimate=cost(2 * nodes * full * full, 2 * full * full),
    )(slope, weight, inverse, upstream, extra, *after)


def left_factor(at_ref, lefts, left_parts, left_sem, left_ref):
    nodes = lefts[0].shape[0]
    width = left_parts.shape[2]
    mine = pl.ds(pl.multiple_of(at_ref[0] % 2 * width, width), width)
    copies = [fetch(ref.at[:, mine], left_parts.at[i], left_sem.at[i]) for i, ref in enumerate(lefts)]

    def finish():
        for i, copy in enumerate(copies):
            copy.wait()
            left_ref[:width, lanes(i, nodes)] = left_parts[i].T
        left_ref[width:, :] = jnp.ones((left_ref.shape[0] - width, left_ref.shape[1]), BF16)

    return finish


def products(at_ref, left_ref, right, copies, width, use):
    bias = jnp.zeros((8, width), F32)
    step = right.shape[1] // len(copies)
    for block, group in enumerate(copies):
        for copy in group:
            copy.wait()
        here = lanes(block, step)
        total = jnp.dot(left_ref[...], right[:, here], preferred_element_type=F32)
        use(here, total)
        for part in range(step // width):
            one = block * (step // width) + part
            bias += jnp.where(at_ref[0] == one, total[width : width + 8, lanes(part, width)], 0.0)
    return bias


def small_sums(bias, stats, rows):
    high, stats_high = bias.astype(BF16).astype(F32), stats.astype(BF16).astype(F32)
    line = lax.broadcasted_iota(jnp.int32, (8, LANES), 0)
    first = jnp.where(line == 0, high, jnp.where(line == 1, bias - high, 0.0))
    rest = jnp.zeros((rows - 24, LANES), F32)
    return jnp.concatenate([first, stats_high, stats - stats_high, rest], axis=0).astype(BF16)


def read_small(extra):
    return extra[0:1] + extra[1:2], extra[8:16] + extra[16:24]


def weight_kernel(masks, at_ref, *refs):
    lefts, rights, outs = refs[:8], refs[8 : -7 - len(masks)], refs[-7 - len(masks) : -7]
    left_parts, left_sem, right, right_sems, stat_parts, stat_sems, left_ref = refs[-7:]
    col = at_ref[1]
    full = outs[0].shape[1] - LANES
    piece_rows = outs[0].shape[0] // len(masks[0])
    pieces = sum(len(group) for group in masks)
    nodes, width = left_parts.shape[1:]
    finish = left_factor(at_ref, lefts, left_parts, left_sem, left_ref)
    steps = right_sems.shape[0]
    starts = [sum(ref.shape[0] for ref in rights[:i]) for i in range(len(rights))]
    copies = [
        [
            fetch(
                ref.at[:, lanes(block, full // steps)],
                right.at[slice(start, start + ref.shape[0]), lanes(block, full // steps)],
                right_sems.at[block, i],
            )
            for i, (ref, start) in enumerate(zip(rights, starts, strict=True))
        ]
        for block in range(steps)
    ]
    firsts = [ref for ref, start in zip(rights, starts, strict=True) if start % nodes == 0]
    stat_copies = [
        fetch(ref.at[:16, slice(full, full + LANES)], stat_parts.at[i], stat_sems.at[i])
        for i, ref in enumerate(firsts)
    ]
    finish()

    def use(here, total):
        for group, ref in zip(masks, outs, strict=True):
            for at, mask in enumerate(group):
                value = total[:piece_rows]
                for piece in range(1, pieces):
                    value = jnp.where(col ^ mask == piece, total[lanes(piece, piece_rows)], value)
                ref[lanes(at, piece_rows), here] = value.astype(BF16)

    bias = products(at_ref, left_ref, right, copies, width, use)
    stats = jnp.zeros((8, LANES), F32)
    for i, copy in enumerate(stat_copies):
        copy.wait()
        both = stat_parts[i].astype(F32)
        stats += both[:8] + both[8:]
    for group, ref in zip(masks, outs, strict=True):
        for at, mask in enumerate(group):
            piece = col ^ mask
            one = jnp.where(piece >= 2, bias[:, LANES:], bias[:, :LANES])
            one = jnp.where(piece % 2 == 1, pltpu.roll(one, LANES // 2, 1), one)
            ref[lanes(at, piece_rows), full:] = small_sums(one, stats, piece_rows)


def weight_product(at, lefts, rights, masks):
    nodes, full = lefts[0].shape[0], rights[0].shape[1]
    full -= LANES
    width = lefts[0].shape[1] // 2
    rows = width // sum(len(group) for group in masks)
    return pl.pallas_call(
        functools.partial(weight_kernel, masks),
        in_specs=[IN_SMEM] + [IN_ANY] * (8 + len(rights)),
        out_specs=[IN_VMEM] * len(masks),
        out_shape=[jax.ShapeDtypeStruct((rows * len(group), full + LANES), BF16) for group in masks],
        scratch_shapes=[
            pltpu.VMEM((8, nodes, width), BF16),
            pltpu.SemaphoreType.DMA((8,)),
            pltpu.VMEM((8 * nodes, full), BF16),
            pltpu.SemaphoreType.DMA((2, len(rights))),
            pltpu.VMEM((8, 16, LANES), BF16),
            pltpu.SemaphoreType.DMA((8,)),
            pltpu.VMEM((width + 16, 8 * nodes), BF16),
        ],
        compiler_params=PARAMS,
        cost_estimate=cost(2 * 8 * nodes * full * width, 4 * 8 * nodes * full),
    )(at, *lefts, *rights)


def pair_kernel(one_ref, two_ref, out_ref):
    rows, full = out_ref.shape
    full -= LANES
    step = 512
    for at in range(0, full, step):
        here = slice(at, at + step)
        out_ref[:, here] = (one_ref[rows:, here].astype(F32) + two_ref[rows:, here].astype(F32)).astype(BF16)
    bias, stats = read_small(one_ref[rows:, full:].astype(F32) + two_ref[rows:, full:].astype(F32))
    out_ref[:, full:] = small_sums(bias, stats, rows)


def pair_sum(one, two):
    return pl.pallas_call(
        pair_kernel,
        in_specs=[IN_VMEM] * 2,
        out_specs=IN_VMEM,
        out_shape=jax.ShapeDtypeStruct((one.shape[0] // 2, one.shape[1]), BF16),
        compiler_params=PARAMS,
    )(one, two)


def sum_kernel(*refs):
    parts, (out_ref, bias_ref, rms_ref) = refs[:-3], refs[-3:]
    rows, full = out_ref.shape
    count = bias_ref.shape[1]

    def total(here):
        return sum([part[:rows, here].astype(F32) for part in parts[1:]], parts[0][:rows, here].astype(F32))

    step = 512
    for at in range(0, full, step):
        out_ref[:, at : at + step] = total(slice(at, at + step))
    bias, stats = read_small(total(slice(full, full + LANES)))
    bias_ref[...] = bias[:, :count]
    rms = jnp.sqrt(stats / jnp.maximum(stats[6:7] * full, 1.0) + 1e-06)
    row = lax.broadcasted_iota(jnp.int32, rms_ref.shape, 0)
    place = 3 * row + lax.broadcasted_iota(jnp.int32, rms_ref.shape, 1)
    value = jnp.zeros(rms_ref.shape, F32)
    for at in range(6):
        value = jnp.where(place == at, rms[at : at + 1, :3], value)
    rms_ref[...] = value


def sum_pieces(parts):
    rows, full = parts[-1].shape
    full -= LANES
    return pl.pallas_call(
        sum_kernel,
        in_specs=[IN_VMEM] * len(parts),
        out_specs=[IN_VMEM] * 3,
        out_shape=[
            jax.ShapeDtypeStruct((rows, full), F32),
            jax.ShapeDtypeStruct((1, rows), F32),
            jax.ShapeDtypeStruct((2, 3), F32),
        ],
        compiler_params=PARAMS,
    )(*parts)


def final_kernel(up_ref, agg_ref, inverse_ref, out_ref):
    inverse = inverse_ref[...]
    for at in range(up_ref.shape[0]):
        value = up_ref[at].astype(F32) + 2.0 * agg_ref[at].astype(F32) * inverse
        out_ref[:, lanes(at)] = value.T.astype(BF16)


def input_gradient(upstream, grad_agg, inverse):
    chips, width, nodes = upstream.shape
    return pl.pallas_call(
        final_kernel,
        in_specs=[IN_VMEM] * 3,
        out_specs=IN_VMEM,
        out_shape=jax.ShapeDtypeStruct((nodes, chips * width), BF16),
        compiler_params=PARAMS,
    )(upstream, grad_agg, inverse)


def transposed(features, weight_one, bias_one, weight_two, bias_two, cotangent, neighbours, valid_mask):
    nodes, full = features.shape
    chip_rows, cols = lax.axis_size("ch"), lax.axis_size("col")
    chips = chip_rows * cols
    core = lax.axis_index("core")
    col = lax.axis_index("col")
    row = (2 * lax.axis_index("ch") + core).reshape(1)
    every = ("ch", "col")

    def swap(value):
        return lax.ppermute(value, "core", [(0, 1), (1, 0)])

    def across(value, mask):
        return lax.ppermute(value, "ch", [(i, i ^ mask) for i in range(chip_rows)])

    def exchange(value):
        return lax.all_to_all(value, every, 0, 0, tiled=True)

    at = jnp.concatenate([row, col.reshape(1)])

    lists = neighbours.reshape(-1, MXU)
    lists = jnp.stack([lists] + [across(lists, mask) for mask in range(1, chip_rows)])
    own = exchange(jnp.transpose(features.reshape(nodes, chips, LANES), (1, 0, 2)))
    turned = count_tile(at, lists, nodes, cols, True)
    tile_own = count_tile(at, lists, nodes, cols, False)
    tile_other = count_tile(at, swap(lists), nodes, cols, False)

    own_lists = lax.dynamic_slice_in_dim(neighbours, col * nodes, nodes, 0)
    inverse = 1.0 / (jnp.sum(own_lists >= 0, axis=1).astype(F32) + 1.0)
    inverse = inverse.reshape(1, nodes)
    valid = valid_mask.astype(F32).reshape(nodes, 1)

    def to_plane(parts):
        return [parts[0]] + [across(parts[mask], mask) for mask in range(1, chip_rows)]

    def both_cores(parts):
        return [part for one in parts for part in (one, swap(one))]

    def along(value, mask):
        return lax.ppermute(value, "col", [(i, i ^ mask) for i in range(cols)])

    def exchange_beside(value, *others):
        return lax.optimization_barrier((exchange(value), *others))

    own, turned = lax.optimization_barrier((own, turned))
    agg_one = exchange(apply_adjacency([turned], own, swap(own), True))
    agg_one, tile_own = lax.optimization_barrier((agg_one, tile_own))
    hidden, slope_one, stats_one, *pieces_one = first_layer(
        at, agg_one, weight_one, bias_one.reshape(1, -1), valid, features, chip_rows
    )
    own, tile_other = exchange_beside(hidden, tile_other)
    agg_two = apply_adjacency([turned], own, swap(own), True)
    agg_two, *pieces_one = exchange_beside(agg_two, *to_plane(pieces_one))
    act, grad_pre_two, sums_two, grad_agg_two, *pieces_two = second_layer(
        at, agg_two, weight_two, bias_two.reshape(1, -1), valid, cotangent, inverse, stats_one, chip_rows
    )
    cut = nodes // 2

    def backward_one(grads, grad_pre, *others):
        own, by_x, by_y, core_other, *others = exchange_beside(
            grads, across(grad_pre, 1), across(grad_pre, 2), swap(grad_pre), *others
        )
        diagonal = across(by_x, 2)
        sums = apply_adjacency([tile_own, tile_other], own, swap(own), False)
        sums, by_x, by_y = lax.optimization_barrier((sums, by_x, by_y))
        return sums, [grad_pre, core_other, *both_cores([by_x, by_y, diagonal])], others

    def backward_two(grads, grad_pre, *others):
        own, by_x, by_y, core_other, *others = exchange_beside(
            grads, across(grad_pre, 1), across(grad_pre, 2), swap(grad_pre), *others
        )
        diagonal = [across(by_x[:cut], 2), across(by_y[cut:], 1)]
        sums = apply_adjacency([tile_own, tile_other], own, swap(own), False)
        sums, by_x, by_y, *diagonal = lax.optimization_barrier((sums, by_x, by_y, *diagonal))
        return sums, [grad_pre, core_other, *both_cores([by_x, by_y]), *both_halves(diagonal)], others

    def both_halves(diagonal):
        return diagonal + [swap(part) for part in diagonal]

    sums, plane_two, _ = backward_two(sums_two, grad_pre_two)
    sums, *pieces_two = lax.optimization_barrier((sums, *pieces_two))
    upstream, *pieces_two = exchange_beside(sums, *to_plane(pieces_two))
    grad_pre_one, sums_one, grad_agg_one = first_layer_back(slope_one, weight_one, inverse, upstream, grad_agg_two)
    kept_two, sent_two = weight_product(at, both_cores(pieces_two), plane_two, ((0, 2), (1, 3)))
    sums, plane_one, (kept_two, sent_two) = backward_one(sums_one, grad_pre_one, kept_two, sent_two)
    grad_start = input_gradient(exchange(sums), grad_agg_one, inverse)
    pair_two = along(sent_two, 1)
    last_two, plane_one[0] = lax.optimization_barrier((pair_sum(kept_two, pair_two), plane_one[0]))
    last_two = along(last_two, 2)
    parts_one = weight_product(at, both_cores(pieces_one), plane_one, tuple((mask,) for mask in range(cols)))
    parts_one = [part if mask == 0 else along(part, mask) for mask, part in enumerate(parts_one)]
    last_two, grad_start = lax.optimization_barrier((last_two, grad_start))
    weight_grad_two, bias_grad_two, rms_stats = sum_pieces([kept_two, pair_two, last_two])
    *parts_one, weight_grad_two = lax.optimization_barrier((*parts_one, weight_grad_two))
    weight_grad_one, bias_grad_one, _ = sum_pieces(parts_one)
    bias_grad_one, bias_grad_two = bias_grad_one.reshape(-1), bias_grad_two.reshape(-1)
    return (act, grad_start, weight_grad_one, bias_grad_one, weight_grad_two, bias_grad_two, rms_stats)


def solution(mesh):
    rows, cols = mesh.devices.shape
    axes = ("ch", "core", "col")
    wide = Mesh(mesh.devices.reshape(rows // 2, 2, cols), axes)

    def program(features, *rest):
        nodes, full = features.shape
        slots = rest[5].shape[1]
        fits = (
            (rows, cols) == (8, 4)
            and nodes == rows * cols * LANES
            and full == rows * cols * 64
            and slots * nodes == MXU * MXU
            and slots == 16
        )
        split, over = (axes, wide) if fits else (("row", "col"), mesh)
        lists = ("ch", "core") if fits else "row"
        spread = P(split, None)
        return jax.shard_map(
            transposed if fits else general,
            mesh=over,
            in_specs=(spread, P(), P(), P(), P(), spread, P(lists, None), P(split)),
            out_specs=(spread, spread, spread, P(split), spread, P(split), P()),
            check_vma=False,
        )(features, *rest)

    return program
```

profile of v0, /device:TPU:8, one launch (start us, length us, event | category | flops | bytes accessed | tf_op | source)
XLA Modules:
  0.0 284.0 jit_solution(17195276283179353534)
XLA Ops:
  1.7 2.5 collective-permute-start.2
  5.2 1.3 copy.19
  6.5 1.0 copy.20
  7.6 7.2 %all-to-all-start = ((bf16[16,128,128]{2,1,0:T(8,128)(2,1)}), bf16[16,128,128]{2,1,0:T(8,128)(2,1)S(1)}, u32[]{:S(2)}, u32[]{:S(2)}) async-start(bf16[16,128,128]{2,1,0:T(8,128)(2,1)} %bitcast.3), calls=%async_computation | async-start | bytes 1048576 | tf_op jit(solution)/shard_map/all_to_all | solution.py:754
  15.0 14.6 %shard_map.135.refs_0_ = f8e4m3fn[4096,2048]{1,0:T(32,128)(4,1)} custom-call(s32[2]{0:T(128)S(1)} %pad_add_fusion.1.place_ref.at_ref, s32[4,32,256]{2,1,0:T(8,128)S(1)} %pad_add_fusion.lists_ref), custom_call_target="tpu_custom_call" | custom-call | flops 17179869184 | bytes 4194304 | tf_op jit(solution)/shard_map/pallas_call | solution.py:237
  29.6 1.9 collective-permute-done.3.other_ref
  31.5 5.8 %shard_map.136 = bf16[16,128,128]{2,1,0:T(8,128)(2,1)} custom-call(bf16[16,128,128]{2,1,0:T(8,128)(2,1)S(1)} %all-to-all-done.own_ref, bf16[16,128,128]{2,1,0:T(8,128)(2,1)S(1)} %collective-permute-done.3.other_ref, f8e4m3fn[4096,2048]{1,0:T(32,128)(4,1)} %shard_map.135.refs_0_), custom_call_target="tpu_custom_call" | custom-call | flops 2147483648 | bytes 8388608 | tf_op jit(solution)/shard_map/pallas_call | solution.py:296
  37.3 6.9 %all-to-all-start.1 = ((bf16[16,128,128]{2,1,0:T(8,128)(2,1)}), bf16[16,128,128]{2,1,0:T(8,128)(2,1)S(1)}, u32[]{:S(2)}, u32[]{:S(2)}) async-start(bf16[16,128,128]{2,1,0:T(8,128)(2,1)} %shard_map.136), calls=%async_computation.1 | async-start | bytes 1048576 | tf_op jit(solution)/shard_map/all_to_all | solution.py:754
  44.4 9.1 %shard_map.137.refs_0_ = f8e4m3fn[2048,2048]{1,0:T(32,128)(4,1)S(1)} custom-call(s32[2]{0:T(128)S(1)} %pad_add_fusion.1.place_ref.at_ref, s32[4,32,256]{2,1,0:T(8,128)S(1)} %pad_add_fusion.lists_ref), custom_call_target="tpu_custom_call" | custom-call | flops 8589934592 | bytes 4194304 | tf_op jit(solution)/shard_map/pallas_call | solution.py:237
  53.5 2.1 copy-done
  55.6 2.2 all-to-all-done.1.agg_ref
  57.8 6.3 %shard_map.138 = (bf16[16,128,128]{2,1,0:T(8,128)(2,1)}, f32[128,2048]{1,0:T(8,128)S(1)}, f32[8,128]{1,0:T(8,128)S(1)}, bf16[128,512]{1,0:T(8,128)(2,1)S(1)}, bf...) custom-call(s32[2]{0:T(128)S(1)} %pad_add_fusion.1.place_ref.at_ref, ...), custom_call_target="tpu_custom_call" | custom-call | flops 1073741824 | bytes 8388608 | tf_op jit(solution)/shard_map/pallas_call | solution.py:378
  64.1 6.4 %all-to-all-start.2 = ((bf16[16,128,128]{2,1,0:T(8,128)(2,1)}), bf16[16,128,128]{2,1,0:T(8,128)(2,1)S(1)}, u32[]{:S(2)}, u32[]{:S(2)}) async-start(bf16[16,128,128]{2,1,0:T(8,128)(2,1)} %get-tuple-element.87), calls=%async_computation.2 | async-start | bytes 1048576 | tf_op jit(solution)/shard_map/all_to_all | solution.py:754
  70.6 1.3 collective-permute-done.4.lists_ref
  71.9 9.1 %shard_map.139.refs_1_ = f8e4m3fn[2048,2048]{1,0:T(32,128)(4,1)S(1)} custom-call(s32[2]{0:T(128)S(1)} %pad_add_fusion.1.place_ref.at_ref, s32[4,32,256]{2,1,0:T(8,128)S(1)} %collective-permute-done.4.lists_ref), custom_call_target="tpu_custom_call" | custom-call | flops 8589934592 | bytes 4194304 | tf_op jit(solution)/shard_map/pallas_call | solution.py:237
  81.0 1.9 copy-done.3
  83.4 1.9 collective-permute-done.5.other_ref
  85.3 5.8 %shard_map.140 = bf16[16,128,128]{2,1,0:T(8,128)(2,1)} custom-call(bf16[16,128,128]{2,1,0:T(8,128)(2,1)S(1)} %all-to-all-done.2.own_ref, bf16[16,128,128]{2,1,0:T(8,128)(2,1)S(1)} %collective-permute-done.5.other_ref, f8e4m3fn[4096,2048]{1,0:T(32,128)(4,1)} %shard_map.135.refs_0_), custom_call_target="tpu_custom_call" | custom-call | flops 2147483648 | bytes 8388608 | tf_op jit(solution)/shard_map/pallas_call | solution.py:296
  91.1 6.6 %all-to-all-start.3 = ((bf16[16,128,128]{2,1,0:T(8,128)(2,1)}), bf16[16,128,128]{2,1,0:T(8,128)(2,1)S(1)}, u32[]{:S(2)}, u32[]{:S(2)}) async-start(bf16[16,128,128]{2,1,0:T(8,128)(2,1)} %shard_map.140), calls=%async_computation.3 | async-start | bytes 1048576 | tf_op jit(solution)/shard_map/all_to_all | solution.py:754
  98.4 1.5 collective-permute-start.6
  99.9 1.5 collective-permute-start.7
  101.9 5.3 %collective-permute-done.6.refs_2_ = bf16[128,512]{1,0:T(8,128)(2,1)S(1)} collective-permute-done((bf16[128,512]{1,0:T(8,128)(2,1)S(1)}, bf16[128,512]{1,0:T(8,128)(2,1)S(1)}, u32[]{:S(2)}, u32[]{:S(2)}) %collective-permute-start.6) | collective-permute-done | bytes 131104 | tf_op jit(solution)/shard_map/ppermute | solution.py:751
  107.2 2.0 collective-permute-done.7.refs_4_
  109.2 2.9 %collective-permute-done.8.refs_6_ = bf16[128,512]{1,0:T(8,128)(2,1)S(1)} collective-permute-done((bf16[128,512]{1,0:T(8,128)(2,1)S(1)}, bf16[128,512]{1,0:T(8,128)(2,1)S(1)}, u32[]{:S(2)}, u32[]{:S(2)}) %collective-permute-start.8) | collective-permute-done | bytes 131104 | tf_op jit(solution)/shard_map/ppermute | solution.py:751
  112.2 11.2 %shard_map.141 = (bf16[128,2048]{1,0:T(8,128)(2,1)}, bf16[128,2176]{1,0:T(8,128)(2,1)}, bf16[16,128,128]{2,1,0:T(8,128)(2,1)}, bf16[16,128,128]{2,1,0:T(8,128)(2...) custom-call(s32[2]{0:T(128)S(1)} %pad_add_fusion.1.place_ref.at_ref,, ...), custom_call_target="tpu_custom_call" | custom-call | flops 2147483648 | bytes 8388608 | tf_op jit(solution)/shard_map/pallas_call | solution.py:466
  126.7 5.6 %all-to-all-start.4 = ((bf16[16,128,128]{2,1,0:T(8,128)(2,1)}), bf16[16,128,128]{2,1,0:T(8,128)(2,1)S(1)}, u32[]{:S(2)}, u32[]{:S(2)}) async-start(bf16[16,128,128]{2,1,0:T(8,128)(2,1)} %get-tuple-element.97), calls=%async_computation.4 | async-start | bytes 1048576 | tf_op jit(solution)/shard_map/all_to_all | solution.py:754
  132.5 1.6 collective-permute-start.10
  134.0 1.5 collective-permute-start.9
  136.3 16.1 %collective-permute-done.10.refs_12_ = bf16[128,2176]{1,0:T(8,128)(2,1)S(1)} collective-permute-done((bf16[128,2176]{1,0:T(8,128)(2,1)}, bf16[128,2176]{1,0:T(8,128)(2,1)S(1)}, u32[]{:S(2)}, u32[]{:S(2)}) %collective-permute-start.10) | collective-permute-done | bytes 557088 | tf_op jit(solution)/shard_map/ppermute | solution.py:751
  152.6 1.5 collective-permute-start.14
  154.6 2.2 copy-done.1
  156.8 4.5 %shard_map.142 = bf16[16,128,128]{2,1,0:T(8,128)(2,1)} custom-call(bf16[16,128,128]{2,1,0:T(8,128)(2,1)S(1)} %all-to-all-done.4.own_ref, bf16[16,128,128]{2,1,0:T(8,128)(2,1)S(1)} %collective-permute-done.12.other_ref, f8e4m3fn[2048,2048]{1,0:T(32,128)(4,1)S(1)} %copy-done.1, f8e4m3fn[2048,2048]{1,0:T(32,128)(4,1)} %copy-done.3), custom_call_target="tpu_custom_call" | custom-call | flops 2147483648 | bytes 8388608 | tf_op jit(solution)/shard_map/pallas_call | solution.py:296
  161.8 1.2 collective-permute-done.13.refs_14_
  163.0 5.2 %all-to-all-start.5 = ((bf16[16,128,128]{2,1,0:T(8,128)(2,1)}), bf16[16,128,128]{2,1,0:T(8,128)(2,1)S(1)}, u32[]{:S(2)}, u32[]{:S(2)}) async-start(bf16[16,128,128]{2,1,0:T(8,128)(2,1)} %shard_map.142), calls=%async_computation.5 | async-start | bytes 1048576 | tf_op jit(solution)/shard_map/all_to_all | solution.py:754
  168.2 1.5 collective-permute-start.15
  169.7 1.5 collective-permute-start.16
  171.7 6.6 %collective-permute-done.15.refs_2_ = bf16[128,512]{1,0:T(8,128)(2,1)S(1)} collective-permute-done((bf16[128,512]{1,0:T(8,128)(2,1)}, bf16[128,512]{1,0:T(8,128)(2,1)S(1)}, u32[]{:S(2)}, u32[]{:S(2)}) %collective-permute-start.15) | collective-permute-done | bytes 131104 | tf_op jit(solution)/shard_map/ppermute | solution.py:751
  179.8 2.0 collective-permute-done.17.refs_6_
  181.9 1.0 copy-done.16
  182.9 6.0 %shard_map.143 = (bf16[128,2176]{1,0:T(8,128)(2,1)S(1)}, bf16[16,128,128]{2,1,0:T(8,128)(2,1)S(1)}, bf16[16,128,128]{2,1,0:T(8,128)(2,1)S(1)}) custom-call(f32[128,2048]{1,0:T(8,128)S(1)} %get-tuple-element.96.slope_ref, bf16[2048,2048]{1,0:T(8,128)(2,1)} %weight_ref.5, f32[1,128]{1,0:T(1,128)S(1)} %divide_bitcast_fusion.inverse_ref, ...), custom_call_target="tpu_custom_call" | custom-call | flops 1073741824 | bytes 8388608 | tf_op jit(solution)/shard_map/pallas_call | solution.py:523
  191.4 6.1 %all-to-all-start.6 = ((bf16[16,128,128]{2,1,0:T(8,128)(2,1)}), bf16[16,128,128]{2,1,0:T(8,128)(2,1)S(1)}, u32[]{:S(2)}, u32[]{:S(2)}) async-start(bf16[16,128,128]{2,1,0:T(8,128)(2,1)} %copy-done.13), calls=%async_computation.6 | async-start | bytes 1048576 | tf_op jit(solution)/shard_map/all_to_all | solution.py:754
  198.6 1.9 collective-permute-done.27.refs_16_
  200.5 1.5 collective-permute-start.19
  201.9 1.5 collective-permute-start.18
  203.9 1.0 collective-permute-done.21.refs_1_
  205.5 1.0 collective-permute-done.23.refs_5_
  206.7 1.1 copy-done.10
  210.5 3.8 %shard_map.144 = (bf16[128,2176]{1,0:T(8,128)(2,1)S(1)}, bf16[128,2176]{1,0:T(8,128)(2,1)S(1)}) custom-call(s32[2]{0:T(128)S(1)} %pad_add_fusion.1.place_ref.at_ref, bf16[128,512]{1,0:T(8,128)(2,1)S(1)} %copy-done.26, bf16[128,512]{1,0:T(8,128)(2,1)S(1)} %collective-permute-done.21.refs_1_, bf16[128,512]{1,0:T(8,128)(2,1)S(1)} %copy-done.28, ...), custom_call_target="tpu_custom_call" | custom-call | flops 1073741824 | bytes 8388608 | tf_op jit(solution)/shard_map/pallas_call | solution.py:642
  215.1 2.5 collective-permute-done.19.refs_12_
  218.8 1.2 collective-permute-start.38
  220.7 2.2 copy-done.2
  222.9 4.5 %shard_map.146 = bf16[16,128,128]{2,1,0:T(8,128)(2,1)} custom-call(bf16[16,128,128]{2,1,0:T(8,128)(2,1)S(1)} %all-to-all-done.6.own_ref, bf16[16,128,128]{2,1,0:T(8,128)(2,1)S(1)} %collective-permute-done.31.other_ref, f8e4m3fn[2048,2048]{1,0:T(32,128)(4,1)S(1)} %copy-done.2, f8e4m3fn[2048,2048]{1,0:T(32,128)(4,1)} %copy-done.3), custom_call_target="tpu_custom_call" | custom-call | flops 2147483648 | bytes 8388608 | tf_op jit(solution)/shard_map/pallas_call | solution.py:296
  227.4 5.7 %all-to-all-start.7 = ((bf16[16,128,128]{2,1,0:T(8,128)(2,1)}), bf16[16,128,128]{2,1,0:T(8,128)(2,1)S(1)}, u32[]{:S(2)}, u32[]{:S(2)}) async-start(bf16[16,128,128]{2,1,0:T(8,128)(2,1)} %shard_map.146), calls=%async_computation.7 | async-start | bytes 1048576 | tf_op jit(solution)/shard_map/all_to_all | solution.py:754
  234.6 1.6 collective-permute-done.32.refs_1_
  236.4 1.4 collective-permute-done.33.refs_3_
  239.4 3.0 %collective-permute-start.30 = (bf16[64,2176]{1,0:T(8,128)(2,1)}, bf16[64,2176]{1,0:T(8,128)(2,1)}, u32[]{:S(2)}, u32[]{:S(2)}) collective-permute-start(bf16[64,2176]{1,0:T(8,128)(2,1)} %shard_map.145), channel_id=1, source_target_pairs={{0,2},{1,3},{2,0},{3,1},{4,6},{5,7},{6,4},{7,5},{8,10},{9,11},{10,... | collective-permute-start | bytes 835592 | tf_op jit(solution)/shard_map/ppermute | solution.py:777
  245.9 4.7 %shard_map.148 = (bf16[64,2176]{1,0:T(8,128)(2,1)S(1)}, bf16[64,2176]{1,0:T(8,128)(2,1)}, bf16[64,2176]{1,0:T(8,128)(2,1)}, bf16[64,2176]{1,0:T(8,128)(2,1)}) custom-call(s32[2]{0:T(128)S(1)} %pad_add_fusion.1.place_ref.at_ref, bf16[128,512]{1,0:T(8,128)(2,1)S(1)} %get-tuple-element.138.refs_0_, bf16[128,512]{1,0:T(8,128)(2,1)S(1)} %collective-permute-done.32.refs_1_, ...), custom_call_target="tpu_custom_call" | custom-call | flops 1073741824 | bytes 8388608 | tf_op jit(solution)/shard_map/pallas_call | solution.py:642
  251.5 3.3 %collective-permute-start.42 = (bf16[64,2176]{1,0:T(8,128)(2,1)}, bf16[64,2176]{1,0:T(8,128)(2,1)S(1)}, u32[]{:S(2)}, u32[]{:S(2)}) collective-permute-start(bf16[64,2176]{1,0:T(8,128)(2,1)} %get-tuple-element.149), channel_id=1, source_target_pairs={{0,3},{1,2},{2,1},{3,0},{4,7},{5,6},{6,5},{7,4},{8,11},{9,10},{10,... | collective-permute-start | bytes 835592 | tf_op jit(solution)/shard_map/ppermute | solution.py:777
  254.9 1.0 copy-done.12
  255.9 1.1 shard_map.147
  257.2 1.8 shard_map.149
  259.0 5.1 %collective-permute-done.40.refs_1_ = bf16[64,2176]{1,0:T(8,128)(2,1)S(1)} collective-permute-done((bf16[64,2176]{1,0:T(8,128)(2,1)}, bf16[64,2176]{1,0:T(8,128)(2,1)S(1)}, u32[]{:S(2)}, u32[]{:S(2)}) %collective-permute-start.40) | collective-permute-done | bytes 278560 | tf_op jit(solution)/shard_map/ppermute | solution.py:777
  264.1 11.0 %collective-permute-done.41.refs_2_ = bf16[64,2176]{1,0:T(8,128)(2,1)S(1)} collective-permute-done((bf16[64,2176]{1,0:T(8,128)(2,1)}, bf16[64,2176]{1,0:T(8,128)(2,1)S(1)}, u32[]{:S(2)}, u32[]{:S(2)}) %collective-permute-start.41) | collective-permute-done | bytes 278560 | tf_op jit(solution)/shard_map/ppermute | solution.py:777
  275.1 7.1 %collective-permute-done.42.refs_3_ = bf16[64,2176]{1,0:T(8,128)(2,1)S(1)} collective-permute-done((bf16[64,2176]{1,0:T(8,128)(2,1)}, bf16[64,2176]{1,0:T(8,128)(2,1)S(1)}, u32[]{:S(2)}, u32[]{:S(2)}) %collective-permute-start.42) | collective-permute-done | bytes 278560 | tf_op jit(solution)/shard_map/ppermute | solution.py:777
  (147 shorter events, 31.2 us)
Async XLA Ops:
  1.7 13.3 %collective-permute-start.2 = (s32[32,256]{1,0:T(8,128)S(1)}, s32[32,256]{1,0:T(8,128)S(1)}, u32[]{:S(2)}, u32[]{:S(2)}) collective-permute-start(s32[32,256]{1,0:T(8,128)S(1)} %reshape.63), channel_id=1, source_target_pairs={{0,24},{8,16},{16,8},{24,0},{1,25},{9,17},{17,9},{25,1},{2,26},{10... | collective-permute-start | bytes 98312 | tf_op jit(solution)/shard_map/ppermute | solution.py:751
  4.2 10.8 %collective-permute-start.1 = (s32[32,256]{1,0:T(8,128)S(1)}, s32[32,256]{1,0:T(8,128)S(1)}, u32[]{:S(2)}, u32[]{:S(2)}) collective-permute-start(s32[32,256]{1,0:T(8,128)S(1)} %reshape.63), channel_id=1, source_target_pairs={{0,16},{8,24},{16,0},{24,8},{1,17},{9,25},{17,1},{25,9},{2,18},{10... | collective-permute-start | bytes 98312 | tf_op jit(solution)/shard_map/ppermute | solution.py:751
  4.7 10.3 %collective-permute-start = (s32[32,256]{1,0:T(8,128)S(1)}, s32[32,256]{1,0:T(8,128)S(1)}, u32[]{:S(2)}, u32[]{:S(2)}) collective-permute-start(s32[32,256]{1,0:T(8,128)S(1)} %reshape.63), channel_id=1, source_target_pairs={{0,8},{8,0},{16,24},{24,16},{1,9},{9,1},{17,25},{25,17},{2,10},{10... | collective-permute-start | bytes 98312 | tf_op jit(solution)/shard_map/ppermute | solution.py:751
  7.6 22.1 %all-to-all-start = ((bf16[16,128,128]{2,1,0:T(8,128)(2,1)}), bf16[16,128,128]{2,1,0:T(8,128)(2,1)S(1)}, u32[]{:S(2)}, u32[]{:S(2)}) async-start(bf16[16,128,128]{2,1,0:T(8,128)(2,1)} %bitcast.3), calls=%async_computation | async-start | bytes 1048576 | tf_op jit(solution)/shard_map/all_to_all | solution.py:754
  29.6 14.6 %copy-start.39 = (s32[128]{0:T(128)S(1)}, s32[128]{0:T(128)}, u32[]{:S(2)}) copy-start(s32[128]{0:T(128)} %param.15) | copy-start | bytes 1540
  29.6 1.9 collective-permute-start.3
  37.3 20.5 %all-to-all-start.1 = ((bf16[16,128,128]{2,1,0:T(8,128)(2,1)}), bf16[16,128,128]{2,1,0:T(8,128)(2,1)S(1)}, u32[]{:S(2)}, u32[]{:S(2)}) async-start(bf16[16,128,128]{2,1,0:T(8,128)(2,1)} %shard_map.136), calls=%async_computation.1 | async-start | bytes 1048576 | tf_op jit(solution)/shard_map/all_to_all | solution.py:754
  44.4 13.4 %copy-start.4 = (bf16[128,2048]{1,0:T(8,128)(2,1)S(1)}, bf16[128,2048]{1,0:T(8,128)(2,1)}, u32[]{:S(2)}) copy-start(bf16[128,2048]{1,0:T(8,128)(2,1)} %input_ref.1) | copy-start | bytes 1572868
  44.4 13.4 %copy-start.31 = (f32[2048]{0:T(1024)S(1)}, f32[2048]{0:T(1024)}, u32[]{:S(2)}) copy-start(f32[2048]{0:T(1024)} %param.10) | copy-start | bytes 24580
  64.1 19.3 %all-to-all-start.2 = ((bf16[16,128,128]{2,1,0:T(8,128)(2,1)}), bf16[16,128,128]{2,1,0:T(8,128)(2,1)S(1)}, u32[]{:S(2)}, u32[]{:S(2)}) async-start(bf16[16,128,128]{2,1,0:T(8,128)(2,1)} %get-tuple-element.87), calls=%async_computation.2 | async-start | bytes 1048576 | tf_op jit(solution)/shard_map/all_to_all | solution.py:754
  70.5 1.4 collective-permute-start.4
  83.0 29.2 %copy-start.14 = (bf16[128,2048]{1,0:T(8,128)(2,1)S(1)}, bf16[128,2048]{1,0:T(8,128)(2,1)}, u32[]{:S(2)}) copy-start(bf16[128,2048]{1,0:T(8,128)(2,1)} %cotangent_ref.1) | copy-start | bytes 1572868
  83.0 29.2 %copy-start.32 = (f32[2048]{0:T(1024)S(1)}, f32[2048]{0:T(1024)}, u32[]{:S(2)}) copy-start(f32[2048]{0:T(1024)} %param.12) | copy-start | bytes 24580
  83.3 1.9 collective-permute-start.5
  91.1 21.1 %all-to-all-start.3 = ((bf16[16,128,128]{2,1,0:T(8,128)(2,1)}), bf16[16,128,128]{2,1,0:T(8,128)(2,1)S(1)}, u32[]{:S(2)}, u32[]{:S(2)}) async-start(bf16[16,128,128]{2,1,0:T(8,128)(2,1)} %shard_map.140), calls=%async_computation.3 | async-start | bytes 1048576 | tf_op jit(solution)/shard_map/all_to_all | solution.py:754
  98.4 8.8 %collective-permute-start.6 = (bf16[128,512]{1,0:T(8,128)(2,1)S(1)}, bf16[128,512]{1,0:T(8,128)(2,1)S(1)}, u32[]{:S(2)}, u32[]{:S(2)}) collective-permute-start(bf16[128,512]{1,0:T(8,128)(2,1)S(1)} %get-tuple-element.90), channel_id=1, source_target_pairs={{0,8},{8,0},{16,24},{24,16},{1,9},{9,1},{17,25},{25,17},{2,10},{10... | collective-permute-start | bytes 393224 | tf_op jit(solution)/shard_map/ppermute | solution.py:751
  99.9 9.3 %collective-permute-start.7 = (bf16[128,512]{1,0:T(8,128)(2,1)S(1)}, bf16[128,512]{1,0:T(8,128)(2,1)S(1)}, u32[]{:S(2)}, u32[]{:S(2)}) collective-permute-start(bf16[128,512]{1,0:T(8,128)(2,1)S(1)} %get-tuple-element.91), channel_id=1, source_target_pairs={{0,16},{8,24},{16,0},{24,8},{1,17},{9,25},{17,1},{25,9},{2,18},{10... | collective-permute-start | bytes 393224 | tf_op jit(solution)/shard_map/ppermute | solution.py:751
  101.3 10.8 %collective-permute-start.8 = (bf16[128,512]{1,0:T(8,128)(2,1)S(1)}, bf16[128,512]{1,0:T(8,128)(2,1)S(1)}, u32[]{:S(2)}, u32[]{:S(2)}) collective-permute-start(bf16[128,512]{1,0:T(8,128)(2,1)S(1)} %get-tuple-element.92), channel_id=1, source_target_pairs={{0,24},{8,16},{16,8},{24,0},{1,25},{9,17},{17,9},{25,1},{2,26},{10... | collective-permute-start | bytes 393224 | tf_op jit(solution)/shard_map/ppermute | solution.py:751
  107.2 74.6 %copy-start.19 = (bf16[128,512]{1,0:T(8,128)(2,1)}, bf16[128,512]{1,0:T(8,128)(2,1)S(1)}, u32[]{:S(2)}) copy-start(bf16[128,512]{1,0:T(8,128)(2,1)S(1)} %collective-permute-done.6.refs_2_) | copy-start | bytes 393220
  109.2 72.6 %copy-start.21 = (bf16[128,512]{1,0:T(8,128)(2,1)}, bf16[128,512]{1,0:T(8,128)(2,1)S(1)}, u32[]{:S(2)}) copy-start(bf16[128,512]{1,0:T(8,128)(2,1)S(1)} %collective-permute-done.7.refs_4_) | copy-start | bytes 393220
  112.1 69.7 %copy-start.23 = (bf16[128,512]{1,0:T(8,128)(2,1)}, bf16[128,512]{1,0:T(8,128)(2,1)S(1)}, u32[]{:S(2)}) copy-start(bf16[128,512]{1,0:T(8,128)(2,1)S(1)} %collective-permute-done.8.refs_6_) | copy-start | bytes 393220
  126.7 25.8 %all-to-all-start.4 = ((bf16[16,128,128]{2,1,0:T(8,128)(2,1)}), bf16[16,128,128]{2,1,0:T(8,128)(2,1)S(1)}, u32[]{:S(2)}, u32[]{:S(2)}) async-start(bf16[16,128,128]{2,1,0:T(8,128)(2,1)} %get-tuple-element.97), calls=%async_computation.4 | async-start | bytes 1048576 | tf_op jit(solution)/shard_map/all_to_all | solution.py:754
  132.4 3.1 %collective-permute-start.11 = (bf16[128,2176]{1,0:T(8,128)(2,1)}, bf16[128,2176]{1,0:T(8,128)(2,1)S(1)}, u32[]{:S(2)}, u32[]{:S(2)}) collective-permute-start(bf16[128,2176]{1,0:T(8,128)(2,1)} %get-tuple-element.98.refs_8_), channel_id=1, source_target_pairs={{0,4},{4,0},{1,5},{5,1},{2,6},{6,2},{3,7},{7,3},{8,12},{12,8},{9,1... | collective-permute-start | bytes 1671176 | tf_op jit(solution)/shard_map/ppermute | solution.py:748
  132.5 20.0 %collective-permute-start.10 = (bf16[128,2176]{1,0:T(8,128)(2,1)}, bf16[128,2176]{1,0:T(8,128)(2,1)S(1)}, u32[]{:S(2)}, u32[]{:S(2)}) collective-permute-start(bf16[128,2176]{1,0:T(8,128)(2,1)} %get-tuple-element.98.refs_8_), channel_id=1, source_target_pairs={{0,16},{8,24},{16,0},{24,8},{1,17},{9,25},{17,1},{25,9},{2,18},{10... | collective-permute-start | bytes 1671176 | tf_op jit(solution)/shard_map/ppermute | solution.py:751
  134.0 18.4 %collective-permute-start.9 = (bf16[128,2176]{1,0:T(8,128)(2,1)}, bf16[128,2176]{1,0:T(8,128)(2,1)S(1)}, u32[]{:S(2)}, u32[]{:S(2)}) collective-permute-start(bf16[128,2176]{1,0:T(8,128)(2,1)} %get-tuple-element.98.refs_8_), channel_id=1, source_target_pairs={{0,8},{8,0},{16,24},{24,16},{1,9},{9,1},{17,25},{25,17},{2,10},{10... | collective-permute-start | bytes 1671176 | tf_op jit(solution)/shard_map/ppermute | solution.py:751
  152.5 2.1 collective-permute-start.12
  152.6 9.2 %collective-permute-start.14 = (bf16[64,2176]{1,0:T(8,128)(2,1)S(1)}, bf16[64,2176]{1,0:T(8,128)(2,1)}, u32[]{:S(2)}, u32[]{:S(2)}) collective-permute-start(bf16[64,2176]{1,0:T(8,128)(2,1)S(1)} %slice.7), channel_id=1, source_target_pairs={{0,8},{8,0},{16,24},{24,16},{1,9},{9,1},{17,25},{25,17},{2,10},{10... | collective-permute-start | bytes 835592 | tf_op jit(solution)/shard_map/ppermute | solution.py:751
  154.1 8.9 %collective-permute-start.13 = (bf16[64,2176]{1,0:T(8,128)(2,1)S(1)}, bf16[64,2176]{1,0:T(8,128)(2,1)}, u32[]{:S(2)}, u32[]{:S(2)}) collective-permute-start(bf16[64,2176]{1,0:T(8,128)(2,1)S(1)} %slice.6), channel_id=1, source_target_pairs={{0,16},{8,24},{16,0},{24,8},{1,17},{9,25},{17,1},{25,9},{2,18},{10... | collective-permute-start | bytes 835592 | tf_op jit(solution)/shard_map/ppermute | solution.py:751
  154.6 2.2 copy-start.1
  163.0 18.8 %all-to-all-start.5 = ((bf16[16,128,128]{2,1,0:T(8,128)(2,1)}), bf16[16,128,128]{2,1,0:T(8,128)(2,1)S(1)}, u32[]{:S(2)}, u32[]{:S(2)}) async-start(bf16[16,128,128]{2,1,0:T(8,128)(2,1)} %shard_map.142), calls=%async_computation.5 | async-start | bytes 1048576 | tf_op jit(solution)/shard_map/all_to_all | solution.py:754
  168.2 10.1 %collective-permute-start.15 = (bf16[128,512]{1,0:T(8,128)(2,1)}, bf16[128,512]{1,0:T(8,128)(2,1)S(1)}, u32[]{:S(2)}, u32[]{:S(2)}) collective-permute-start(bf16[128,512]{1,0:T(8,128)(2,1)} %copy-done.36), channel_id=1, source_target_pairs={{0,8},{8,0},{16,24},{24,16},{1,9},{9,1},{17,25},{25,17},{2,10},{10... | collective-permute-start | bytes 393224 | tf_op jit(solution)/shard_map/ppermute | solution.py:751
  169.7 9.4 %collective-permute-start.16 = (bf16[128,512]{1,0:T(8,128)(2,1)}, bf16[128,512]{1,0:T(8,128)(2,1)S(1)}, u32[]{:S(2)}, u32[]{:S(2)}) collective-permute-start(bf16[128,512]{1,0:T(8,128)(2,1)} %copy-done.35), channel_id=1, source_target_pairs={{0,16},{8,24},{16,0},{24,8},{1,17},{9,25},{17,1},{25,9},{2,18},{10... | collective-permute-start | bytes 393224 | tf_op jit(solution)/shard_map/ppermute | solution.py:751
  171.2 10.7 %collective-permute-start.17 = (bf16[128,512]{1,0:T(8,128)(2,1)}, bf16[128,512]{1,0:T(8,128)(2,1)}, u32[]{:S(2)}, u32[]{:S(2)}) collective-permute-start(bf16[128,512]{1,0:T(8,128)(2,1)} %copy-done.34), channel_id=1, source_target_pairs={{0,24},{8,16},{16,8},{24,0},{1,25},{9,17},{17,9},{25,1},{2,26},{10... | collective-permute-start | bytes 393224 | tf_op jit(solution)/shard_map/ppermute | solution.py:751
  178.3 3.5 %copy-start.27 = (bf16[128,512]{1,0:T(8,128)(2,1)}, bf16[128,512]{1,0:T(8,128)(2,1)S(1)}, u32[]{:S(2)}) copy-start(bf16[128,512]{1,0:T(8,128)(2,1)S(1)} %collective-permute-done.15.refs_2_) | copy-start | bytes 393220
  191.4 27.4 %all-to-all-start.6 = ((bf16[16,128,128]{2,1,0:T(8,128)(2,1)}), bf16[16,128,128]{2,1,0:T(8,128)(2,1)S(1)}, u32[]{:S(2)}, u32[]{:S(2)}) async-start(bf16[16,128,128]{2,1,0:T(8,128)(2,1)} %copy-done.13), calls=%async_computation.6 | async-start | bytes 1048576 | tf_op jit(solution)/shard_map/all_to_all | solution.py:754
  197.4 6.0 %collective-permute-start.25 = (bf16[128,2176]{1,0:T(8,128)(2,1)S(1)}, bf16[128,2176]{1,0:T(8,128)(2,1)S(1)}, u32[]{:S(2)}, u32[]{:S(2)}) collective-permute-start(bf16[128,2176]{1,0:T(8,128)(2,1)S(1)} %collective-permute-done.9.refs_10_), channel_id=1, source_target_pairs={{0,4},{4,0},{1,5},{5,1},{2,6},{6,2},{3,7},{7,3},{8,12},{12,8},{9,1... | collective-permute-start | bytes 1671176 | tf_op jit(solution)/shard_map/ppermute | solution.py:748
  197.5 5.9 %collective-permute-start.26 = (bf16[128,2176]{1,0:T(8,128)(2,1)S(1)}, bf16[128,2176]{1,0:T(8,128)(2,1)S(1)}, u32[]{:S(2)}, u32[]{:S(2)}) collective-permute-start(bf16[128,2176]{1,0:T(8,128)(2,1)S(1)} %collective-permute-done.10.refs_12_), channel_id=1, source_target_pairs={{0,4},{4,0},{1,5},{5,1},{2,6},{6,2},{3,7},{7,3},{8,12},{12,8},{9,1... | collective-permute-start | bytes 1671176 | tf_op jit(solution)/shard_map/ppermute | solution.py:748
  198.0 2.5 collective-permute-start.27
  198.1 3.8 %collective-permute-start.28 = (bf16[64,2176]{1,0:T(8,128)(2,1)}, bf16[64,2176]{1,0:T(8,128)(2,1)S(1)}, u32[]{:S(2)}, u32[]{:S(2)}) collective-permute-start(bf16[64,2176]{1,0:T(8,128)(2,1)} %collective-permute-done.14.refs_15_), channel_id=1, source_target_pairs={{0,4},{4,0},{1,5},{5,1},{2,6},{6,2},{3,7},{7,3},{8,12},{12,8},{9,1... | collective-permute-start | bytes 835592 | tf_op jit(solution)/shard_map/ppermute | solution.py:748
  198.5 44.7 %copy-start.6 = (bf16[128,2176]{1,0:T(8,128)(2,1)S(1)}, bf16[128,2176]{1,0:T(8,128)(2,1)}, u32[]{:S(2)}) copy-start(bf16[128,2176]{1,0:T(8,128)(2,1)} %copy-done.5) | copy-start | bytes 1671172
  198.5 16.6 %collective-permute-start.20 = (bf16[128,2176]{1,0:T(8,128)(2,1)}, bf16[128,2176]{1,0:T(8,128)(2,1)S(1)}, u32[]{:S(2)}, u32[]{:S(2)}) collective-permute-start(bf16[128,2176]{1,0:T(8,128)(2,1)} %copy-done.5), channel_id=1, source_target_pairs={{0,4},{4,0},{1,5},{5,1},{2,6},{6,2},{3,7},{7,3},{8,12},{12,8},{9,1... | collective-permute-start | bytes 1671176 | tf_op jit(solution)/shard_map/ppermute | solution.py:748
  200.5 17.1 %collective-permute-start.19 = (bf16[128,2176]{1,0:T(8,128)(2,1)}, bf16[128,2176]{1,0:T(8,128)(2,1)S(1)}, u32[]{:S(2)}, u32[]{:S(2)}) collective-permute-start(bf16[128,2176]{1,0:T(8,128)(2,1)} %copy-done.5), channel_id=1, source_target_pairs={{0,16},{8,24},{16,0},{24,8},{1,17},{9,25},{17,1},{25,9},{2,18},{10... | collective-permute-start | bytes 1671176 | tf_op jit(solution)/shard_map/ppermute | solution.py:751
  201.9 16.8 %collective-permute-start.18 = (bf16[128,2176]{1,0:T(8,128)(2,1)}, bf16[128,2176]{1,0:T(8,128)(2,1)}, u32[]{:S(2)}, u32[]{:S(2)}) collective-permute-start(bf16[128,2176]{1,0:T(8,128)(2,1)} %copy-done.5), channel_id=1, source_target_pairs={{0,8},{8,0},{16,24},{24,16},{1,9},{9,1},{17,25},{25,17},{2,10},{10... | collective-permute-start | bytes 1671176 | tf_op jit(solution)/shard_map/ppermute | solution.py:751
  203.4 1.6 collective-permute-start.21
  203.4 3.3 %copy-start.37 = (bf16[128,2176]{1,0:T(8,128)(2,1)}, bf16[128,2176]{1,0:T(8,128)(2,1)S(1)}, u32[]{:S(2)}) copy-start(bf16[128,2176]{1,0:T(8,128)(2,1)S(1)} %collective-permute-done.26.refs_13_) | copy-start | bytes 1671172
  203.4 1.7 collective-permute-start.22
  205.0 1.6 collective-permute-start.23
  205.2 1.6 collective-permute-start.24
  218.8 1.9 collective-permute-start.31
  218.8 15.4 %collective-permute-start.38 = (bf16[128,2176]{1,0:T(8,128)(2,1)}, bf16[128,2176]{1,0:T(8,128)(2,1)}, u32[]{:S(2)}, u32[]{:S(2)}) collective-permute-start(bf16[128,2176]{1,0:T(8,128)(2,1)} %collective-permute-done.18.refs_10_), channel_id=1, source_target_pairs={{0,16},{8,24},{16,0},{24,8},{1,17},{9,25},{17,1},{25,9},{2,18},{10... | collective-permute-start | bytes 1671176 | tf_op jit(solution)/shard_map/ppermute | solution.py:751
  220.0 18.0 %collective-permute-start.29 = (bf16[128,2176]{1,0:T(8,128)(2,1)}, bf16[128,2176]{1,0:T(8,128)(2,1)S(1)}, u32[]{:S(2)}, u32[]{:S(2)}) collective-permute-start(bf16[128,2176]{1,0:T(8,128)(2,1)} %copy-done.33), channel_id=1, source_target_pairs={{0,1},{1,0},{2,3},{3,2},{4,5},{5,4},{6,7},{7,6},{8,9},{9,8},{10,11... | collective-permute-start | bytes 1671176 | tf_op jit(solution)/shard_map/ppermute | solution.py:777
  222.9 10.3 %copy-start.8 = (bf16[128,2176]{1,0:T(8,128)(2,1)S(1)}, bf16[128,2176]{1,0:T(8,128)(2,1)}, u32[]{:S(2)}) copy-start(bf16[128,2176]{1,0:T(8,128)(2,1)} %copy-done.7) | copy-start | bytes 1671172
  227.4 27.5 %all-to-all-start.7 = ((bf16[16,128,128]{2,1,0:T(8,128)(2,1)}), bf16[16,128,128]{2,1,0:T(8,128)(2,1)S(1)}, u32[]{:S(2)}, u32[]{:S(2)}) async-start(bf16[16,128,128]{2,1,0:T(8,128)(2,1)} %shard_map.146), calls=%async_computation.7 | async-start | bytes 1048576 | tf_op jit(solution)/shard_map/all_to_all | solution.py:754
  233.1 9.2 %collective-permute-start.36 = (bf16[128,2176]{1,0:T(8,128)(2,1)}, bf16[128,2176]{1,0:T(8,128)(2,1)S(1)}, u32[]{:S(2)}, u32[]{:S(2)}) collective-permute-start(bf16[128,2176]{1,0:T(8,128)(2,1)} %collective-permute-done.18.refs_10_), channel_id=1, source_target_pairs={{0,4},{4,0},{1,5},{5,1},{2,6},{6,2},{3,7},{7,3},{8,12},{12,8},{9,1... | collective-permute-start | bytes 1671176 | tf_op jit(solution)/shard_map/ppermute | solution.py:748
  233.2 9.2 %collective-permute-start.37 = (bf16[128,2176]{1,0:T(8,128)(2,1)S(1)}, bf16[128,2176]{1,0:T(8,128)(2,1)S(1)}, u32[]{:S(2)}, u32[]{:S(2)}) collective-permute-start(bf16[128,2176]{1,0:T(8,128)(2,1)S(1)} %copy-done.8), channel_id=1, source_target_pairs={{0,4},{4,0},{1,5},{5,1},{2,6},{6,2},{3,7},{7,3},{8,12},{12,8},{9,1... | collective-permute-start | bytes 1671176 | tf_op jit(solution)/shard_map/ppermute | solution.py:748
  234.1 8.3 %collective-permute-start.39 = (bf16[128,2176]{1,0:T(8,128)(2,1)}, bf16[128,2176]{1,0:T(8,128)(2,1)S(1)}, u32[]{:S(2)}, u32[]{:S(2)}) collective-permute-start(bf16[128,2176]{1,0:T(8,128)(2,1)} %collective-permute-done.38.refs_14_), channel_id=1, source_target_pairs={{0,4},{4,0},{1,5},{5,1},{2,6},{6,2},{3,7},{7,3},{8,12},{12,8},{9,1... | collective-permute-start | bytes 1671176 | tf_op jit(solution)/shard_map/ppermute | solution.py:748
  234.1 2.1 collective-permute-start.32
  236.3 1.6 collective-permute-start.33
  237.8 1.6 collective-permute-start.34
  238.0 4.4 %collective-permute-start.35 = (bf16[128,512]{1,0:T(8,128)(2,1)}, bf16[128,512]{1,0:T(8,128)(2,1)S(1)}, u32[]{:S(2)}, u32[]{:S(2)}) collective-permute-start(bf16[128,512]{1,0:T(8,128)(2,1)} %copy-done.23), channel_id=1, source_target_pairs={{0,4},{4,0},{1,5},{5,1},{2,6},{6,2},{3,7},{7,3},{8,12},{12,8},{9,1... | collective-permute-start | bytes 393224 | tf_op jit(solution)/shard_map/ppermute | solution.py:748
  239.4 17.8 %collective-permute-start.30 = (bf16[64,2176]{1,0:T(8,128)(2,1)}, bf16[64,2176]{1,0:T(8,128)(2,1)}, u32[]{:S(2)}, u32[]{:S(2)}) collective-permute-start(bf16[64,2176]{1,0:T(8,128)(2,1)} %shard_map.145), channel_id=1, source_target_pairs={{0,2},{1,3},{2,0},{3,1},{4,6},{5,7},{6,4},{7,5},{8,10},{9,11},{10,... | collective-permute-start | bytes 835592 | tf_op jit(solution)/shard_map/ppermute | solution.py:777
  251.4 12.7 %collective-permute-start.40 = (bf16[64,2176]{1,0:T(8,128)(2,1)}, bf16[64,2176]{1,0:T(8,128)(2,1)S(1)}, u32[]{:S(2)}, u32[]{:S(2)}) collective-permute-start(bf16[64,2176]{1,0:T(8,128)(2,1)} %get-tuple-element.147), channel_id=1, source_target_pairs={{0,1},{1,0},{2,3},{3,2},{4,5},{5,4},{6,7},{7,6},{8,9},{9,8},{10,11... | collective-permute-start | bytes 835592 | tf_op jit(solution)/shard_map/ppermute | solution.py:777
  251.4 23.7 %collective-permute-start.41 = (bf16[64,2176]{1,0:T(8,128)(2,1)}, bf16[64,2176]{1,0:T(8,128)(2,1)S(1)}, u32[]{:S(2)}, u32[]{:S(2)}) collective-permute-start(bf16[64,2176]{1,0:T(8,128)(2,1)} %get-tuple-element.148), channel_id=1, source_target_pairs={{0,2},{1,3},{2,0},{3,1},{4,6},{5,7},{6,4},{7,5},{8,10},{9,11},{10,... | collective-permute-start | bytes 835592 | tf_op jit(solution)/shard_map/ppermute | solution.py:777
  251.5 30.6 %collective-permute-start.42 = (bf16[64,2176]{1,0:T(8,128)(2,1)}, bf16[64,2176]{1,0:T(8,128)(2,1)S(1)}, u32[]{:S(2)}, u32[]{:S(2)}) collective-permute-start(bf16[64,2176]{1,0:T(8,128)(2,1)} %get-tuple-element.149), channel_id=1, source_target_pairs={{0,3},{1,2},{2,1},{3,0},{4,7},{5,6},{6,5},{7,4},{8,11},{9,10},{10,... | collective-permute-start | bytes 835592 | tf_op jit(solution)/shard_map/ppermute | solution.py:777
  (27 other events, 26.1 us)
where the time goes:
time: 286 us; the launch traced here: 284 us
  Pallas kernels  90.1 us (32%)
  starting transfers between devices  80.2 us (28%)
  waiting for transfers between devices  79.9 us (28%)
  local copies, waits for them, and re-layouts  31.9 us (11%)
    all_to_all x8, starting transfers between devices, exchange(): return lax.all_to_all(value, every, 0, 0, tiled=True)  50 us
    ppermute x16, waiting for transfers between devices, across(): return lax.ppermute(value, 'ch', [(i, i ^ mask) for i in range(chip_rows)])  40.7 us
    pallas_call x3, Pallas kernels, count_tile(): pl.pallas_call(functools.partial(tile_kernel, turn, nodes, cols), grid=(r...  32.8 us
    unnamed x82, local copies, waits for them, and re-layouts  30.4 us
    ppermute x5, waiting for transfers between devices, along(): return lax.ppermute(value, 'col', [(i, i ^ mask) for i in range(cols)])  23.3 us
    pallas_call x4, Pallas kernels, apply_adjacency(): pl.pallas_call(functools.partial(adjacency_kernel, forward, len(tiles)),...  20.6 us
    ppermute x16, starting transfers between devices, across(): return lax.ppermute(value, 'ch', [(i, i ^ mask) for i in range(chip_rows)])  19.8 us
    ppermute x22, waiting for transfers between devices, swap(): return lax.ppermute(value, 'core', [(0, 1), (1, 0)])  13.3 us
  transfers between devices with their start and end apart: 51, of which 29 were waited for; matrix products, arithmetic and copies ran while one was open for 1% of the time, Pallas kernels for 19%

commit v1 on v0

--- a/solution.py
+++ b/solution.py
@@ -131,7 +131,8 @@
 IN_SMEM = pl.BlockSpec(memory_space=pltpu.SMEM)
 IN_ANY = pl.BlockSpec(memory_space=pl.ANY)
 COUNT = jnp.float8_e4m3fn
-PARAMS = pltpu.CompilerParams(vmem_limit_bytes=48 * MIB)
+PARAMS = pltpu.CompilerParams(vmem_limit_bytes=51 * MIB)
+WIDE = pltpu.CompilerParams(vmem_limit_bytes=62 * MIB)
 
 
 def cost(flops, read, transcendentals=0):
@@ -486,7 +487,7 @@
             pltpu.VMEM((chip_rows,) + pieces[0].shape, BF16),
             pltpu.SemaphoreType.DMA((chip_rows + steps + 1 + 8,)),
         ],
-        compiler_params=PARAMS,
+        compiler_params=WIDE,
         cost_estimate=cost(4 * nodes * full * full, 2 * full * full, nodes * full),
     )(at, agg, weight, bias, valid, cotangent, inverse, stats, *after)
 

time: 286 us -> 277 us (0.969)
  local copies, waits for them, and re-layouts: 31.9 us -> 13.1 us
  waiting for transfers between devices: 79.9 us -> 86.2 us
  Pallas kernels: 90.1 us -> 95.5 us
    unnamed x82 -> x68, local copies, waits for them, and re-layouts: 30.4 us -> 11.6 us
    ppermute x16, waiting for transfers between devices: 40.7 us -> 45.5 us  [across(): return lax.ppermute(value, 'ch', [(i, i ^ mask) for i in range(chip_rows)])]
    pallas_call x3, Pallas kernels: 32.8 us -> 36.6 us  [count_tile(): pl.pallas_call(functools.partial(tile_kernel, turn, nodes, cols), grid=(r...]
  transfers between devices with their start and end apart: 51 -> 51, of which waited for: 29 -> 29; matrix products, arithmetic and copies ran while one was open for 1% -> 1% of each run, Pallas kernels for 19% -> 22%
where the time goes in v1:
time: 277 us; the launch traced here: 275 us
  Pallas kernels  95.5 us (34%)
  waiting for transfers between devices  86.2 us (31%)
  starting transfers between devices  78.1 us (28%)
  local copies, waits for them, and re-layouts  13.1 us (5%)
    all_to_all x8, starting transfers between devices, exchange(): return lax.all_to_all(value, every, 0, 0, tiled=True)  49.1 us
    ppermute x16, waiting for transfers between devices, across(): return lax.ppermute(value, 'ch', [(i, i ^ mask) for i in range(chip_rows)])  45.5 us
    pallas_call x3, Pallas kernels, count_tile(): pl.pallas_call(functools.partial(tile_kernel, turn, nodes, cols), grid=(r...  36.6 us
    ppermute x5, waiting for transfers between devices, along(): return lax.ppermute(value, 'col', [(i, i ^ mask) for i in range(cols)])  24.9 us
    pallas_call x4, Pallas kernels, apply_adjacency(): pl.pallas_call(functools.partial(adjacency_kernel, forward, len(tiles)),...  22.6 us
    ppermute x16, starting transfers between devices, across(): return lax.ppermute(value, 'ch', [(i, i ^ mask) for i in range(chip_rows)])  20 us
    ppermute x22, waiting for transfers between devices, swap(): return lax.ppermute(value, 'core', [(0, 1), (1, 0)])  12.9 us
    unnamed x68, local copies, waits for them, and re-layouts  11.6 us
  transfers between devices with their start and end apart: 51, of which 29 were waited for; matrix products, arithmetic and copies ran while one was open for 1% of the time, Pallas kernels for 22%

profile of v1, /device:TPU:8, one launch (start us, length us, event | category | flops | bytes accessed | tf_op | source)
XLA Modules:
  0.0 275.2 jit_solution(3796883788154692156)
XLA Ops:
  1.7 2.5 collective-permute-start.2
  5.2 1.3 copy.19
  6.5 1.0 copy.20
  7.6 7.2 %all-to-all-start = ((bf16[16,128,128]{2,1,0:T(8,128)(2,1)}), bf16[16,128,128]{2,1,0:T(8,128)(2,1)S(1)}, u32[]{:S(2)}, u32[]{:S(2)}) async-start(bf16[16,128,128]{2,1,0:T(8,128)(2,1)} %bitcast.3), calls=%async_computation | async-start | bytes 1048576 | tf_op jit(solution)/shard_map/all_to_all | solution.py:755
  15.0 14.6 %shard_map.135.refs_0_ = f8e4m3fn[4096,2048]{1,0:T(32,128)(4,1)} custom-call(s32[2]{0:T(128)S(1)} %pad_add_fusion.1.place_ref.at_ref, s32[4,32,256]{2,1,0:T(8,128)S(1)} %pad_add_fusion.lists_ref), custom_call_target="tpu_custom_call" | custom-call | flops 17179869184 | bytes 4194304 | tf_op jit(solution)/shard_map/pallas_call | solution.py:238
  29.7 1.9 collective-permute-done.3.other_ref
  31.6 5.8 %shard_map.136 = bf16[16,128,128]{2,1,0:T(8,128)(2,1)} custom-call(bf16[16,128,128]{2,1,0:T(8,128)(2,1)S(1)} %all-to-all-done.own_ref, bf16[16,128,128]{2,1,0:T(8,128)(2,1)S(1)} %collective-permute-done.3.other_ref, f8e4m3fn[4096,2048]{1,0:T(32,128)(4,1)} %shard_map.135.refs_0_), custom_call_target="tpu_custom_call" | custom-call | flops 2147483648 | bytes 8388608 | tf_op jit(solution)/shard_map/pallas_call | solution.py:297
  37.4 6.9 %all-to-all-start.1 = ((bf16[16,128,128]{2,1,0:T(8,128)(2,1)}), bf16[16,128,128]{2,1,0:T(8,128)(2,1)S(1)}, u32[]{:S(2)}, u32[]{:S(2)}) async-start(bf16[16,128,128]{2,1,0:T(8,128)(2,1)} %shard_map.136), calls=%async_computation.1 | async-start | bytes 1048576 | tf_op jit(solution)/shard_map/all_to_all | solution.py:755
  44.4 11.0 %shard_map.137.refs_0_ = f8e4m3fn[2048,2048]{1,0:T(32,128)(4,1)} custom-call(s32[2]{0:T(128)S(1)} %pad_add_fusion.1.place_ref.at_ref, s32[4,32,256]{2,1,0:T(8,128)S(1)} %pad_add_fusion.lists_ref), custom_call_target="tpu_custom_call" | custom-call | flops 8589934592 | bytes 4194304 | tf_op jit(solution)/shard_map/pallas_call | solution.py:238
  55.4 2.4 all-to-all-done.1.agg_ref
  57.8 6.4 %shard_map.138 = (bf16[16,128,128]{2,1,0:T(8,128)(2,1)}, f32[128,2048]{1,0:T(8,128)}, f32[8,128]{1,0:T(8,128)S(1)}, bf16[128,512]{1,0:T(8,128)(2,1)S(1)}, bf16[1...) custom-call(s32[2]{0:T(128)S(1)} %pad_add_fusion.1.place_ref.at_ref, ...), custom_call_target="tpu_custom_call" | custom-call | flops 1073741824 | bytes 8388608 | tf_op jit(solution)/shard_map/pallas_call | solution.py:379
  64.2 6.4 %all-to-all-start.2 = ((bf16[16,128,128]{2,1,0:T(8,128)(2,1)}), bf16[16,128,128]{2,1,0:T(8,128)(2,1)S(1)}, u32[]{:S(2)}, u32[]{:S(2)}) async-start(bf16[16,128,128]{2,1,0:T(8,128)(2,1)} %get-tuple-element.87), calls=%async_computation.2 | async-start | bytes 1048576 | tf_op jit(solution)/shard_map/all_to_all | solution.py:755
  70.7 1.3 collective-permute-done.4.lists_ref
  72.1 11.0 %shard_map.139.refs_1_ = f8e4m3fn[2048,2048]{1,0:T(32,128)(4,1)} custom-call(s32[2]{0:T(128)S(1)} %pad_add_fusion.1.place_ref.at_ref, s32[4,32,256]{2,1,0:T(8,128)S(1)} %collective-permute-done.4.lists_ref), custom_call_target="tpu_custom_call" | custom-call | flops 8589934592 | bytes 4194304 | tf_op jit(solution)/shard_map/pallas_call | solution.py:238
  83.5 1.9 collective-permute-done.5.other_ref
  85.4 5.8 %shard_map.140 = bf16[16,128,128]{2,1,0:T(8,128)(2,1)} custom-call(bf16[16,128,128]{2,1,0:T(8,128)(2,1)S(1)} %all-to-all-done.2.own_ref, bf16[16,128,128]{2,1,0:T(8,128)(2,1)S(1)} %collective-permute-done.5.other_ref, f8e4m3fn[4096,2048]{1,0:T(32,128)(4,1)} %shard_map.135.refs_0_), custom_call_target="tpu_custom_call" | custom-call | flops 2147483648 | bytes 8388608 | tf_op jit(solution)/shard_map/pallas_call | solution.py:297
  91.2 6.6 %all-to-all-start.3 = ((bf16[16,128,128]{2,1,0:T(8,128)(2,1)}), bf16[16,128,128]{2,1,0:T(8,128)(2,1)S(1)}, u32[]{:S(2)}, u32[]{:S(2)}) async-start(bf16[16,128,128]{2,1,0:T(8,128)(2,1)} %shard_map.140), calls=%async_computation.3 | async-start | bytes 1048576 | tf_op jit(solution)/shard_map/all_to_all | solution.py:755
  98.5 1.5 collective-permute-start.6
  99.9 1.5 collective-permute-start.7
  102.5 4.8 %collective-permute-done.6.refs_2_ = bf16[128,512]{1,0:T(8,128)(2,1)S(1)} collective-permute-done((bf16[128,512]{1,0:T(8,128)(2,1)S(1)}, bf16[128,512]{1,0:T(8,128)(2,1)S(1)}, u32[]{:S(2)}, u32[]{:S(2)}) %collective-permute-start.6) | collective-permute-done | bytes 131104 | tf_op jit(solution)/shard_map/ppermute | solution.py:752
  107.3 2.2 collective-permute-done.7.refs_4_
  109.5 2.9 %collective-permute-done.8.refs_6_ = bf16[128,512]{1,0:T(8,128)(2,1)} collective-permute-done((bf16[128,512]{1,0:T(8,128)(2,1)S(1)}, bf16[128,512]{1,0:T(8,128)(2,1)}, u32[]{:S(2)}, u32[]{:S(2)}) %collective-permute-start.8) | collective-permute-done | bytes 131104 | tf_op jit(solution)/shard_map/ppermute | solution.py:752
  113.2 9.1 %shard_map.141 = (bf16[128,2048]{1,0:T(8,128)(2,1)}, bf16[128,2176]{1,0:T(8,128)(2,1)}, bf16[16,128,128]{2,1,0:T(8,128)(2,1)}, bf16[16,128,128]{2,1,0:T(8,128)(2...) custom-call(s32[2]{0:T(128)} %copy-done.15, ...), custom_call_target="tpu_custom_call" | custom-call | flops 2147483648 | bytes 8388608 | tf_op jit(solution)/shard_map/pallas_call | solution.py:467
  122.3 5.7 %all-to-all-start.4 = ((bf16[16,128,128]{2,1,0:T(8,128)(2,1)}), bf16[16,128,128]{2,1,0:T(8,128)(2,1)S(1)}, u32[]{:S(2)}, u32[]{:S(2)}) async-start(bf16[16,128,128]{2,1,0:T(8,128)(2,1)} %get-tuple-element.97), calls=%async_computation.4 | async-start | bytes 1048576 | tf_op jit(solution)/shard_map/all_to_all | solution.py:755
  128.0 1.6 collective-permute-start.10
  129.6 1.5 collective-permute-start.9
  131.1 17.0 %collective-permute-done.10.refs_12_ = bf16[128,2176]{1,0:T(8,128)(2,1)S(1)} collective-permute-done((bf16[128,2176]{1,0:T(8,128)(2,1)}, bf16[128,2176]{1,0:T(8,128)(2,1)S(1)}, u32[]{:S(2)}, u32[]{:S(2)}) %collective-permute-start.10) | collective-permute-done | bytes 557088 | tf_op jit(solution)/shard_map/ppermute | solution.py:752
  148.3 1.6 collective-permute-start.14
  150.4 5.5 %shard_map.142 = bf16[16,128,128]{2,1,0:T(8,128)(2,1)} custom-call(bf16[16,128,128]{2,1,0:T(8,128)(2,1)S(1)} %all-to-all-done.4.own_ref, bf16[16,128,128]{2,1,0:T(8,128)(2,1)S(1)} %collective-permute-done.12.other_ref, f8e4m3fn[2048,2048]{1,0:T(32,128)(4,1)} %shard_map.137.refs_0_, f8e4m3fn[2048,2048]{1,0:T(32,128)(4,1)} %shard_map.139.refs_1_), custom_call_target="tpu_custom_call" | custom-call | flops 2147483648 | bytes 8388608 | tf_op jit(solution)/shard_map/pallas_call | solution.py:297
  155.9 1.5 collective-permute-done.14.refs_15_
  157.4 1.2 collective-permute-done.13.refs_14_
  158.6 5.2 %all-to-all-start.5 = ((bf16[16,128,128]{2,1,0:T(8,128)(2,1)}), bf16[16,128,128]{2,1,0:T(8,128)(2,1)S(1)}, u32[]{:S(2)}, u32[]{:S(2)}) async-start(bf16[16,128,128]{2,1,0:T(8,128)(2,1)} %shard_map.142), calls=%async_computation.5 | async-start | bytes 1048576 | tf_op jit(solution)/shard_map/all_to_all | solution.py:755
  163.8 1.5 collective-permute-start.15
  165.3 1.5 collective-permute-start.16
  167.3 6.5 %collective-permute-done.15.refs_2_ = bf16[128,512]{1,0:T(8,128)(2,1)S(1)} collective-permute-done((bf16[128,512]{1,0:T(8,128)(2,1)}, bf16[128,512]{1,0:T(8,128)(2,1)S(1)}, u32[]{:S(2)}, u32[]{:S(2)}) %collective-permute-start.15) | collective-permute-done | bytes 131104 | tf_op jit(solution)/shard_map/ppermute | solution.py:752
  173.9 1.9 collective-permute-done.16.refs_4_
  175.7 1.6 collective-permute-done.17.refs_6_
  177.3 7.0 %shard_map.143 = (bf16[128,2176]{1,0:T(8,128)(2,1)S(1)}, bf16[16,128,128]{2,1,0:T(8,128)(2,1)}, bf16[16,128,128]{2,1,0:T(8,128)(2,1)S(1)}) custom-call(f32[128,2048]{1,0:T(8,128)} %get-tuple-element.96.slope_ref, bf16[2048,2048]{1,0:T(8,128)(2,1)} %weight_ref.5, f32[1,128]{1,0:T(1,128)S(1)} %copy-done.18, bf16[16,128,128]{2,1,0:T(8,128)(2,1)S(1)} %all-to-all-done.5.up_ref, ...), custom_call_target="tpu_custom_call" | custom-call | flops 1073741824 | bytes 8388608 | tf_op jit(solution)/shard_map/pallas_call | solution.py:524
  184.4 5.7 %all-to-all-start.6 = ((bf16[16,128,128]{2,1,0:T(8,128)(2,1)}), bf16[16,128,128]{2,1,0:T(8,128)(2,1)S(1)}, u32[]{:S(2)}, u32[]{:S(2)}) async-start(bf16[16,128,128]{2,1,0:T(8,128)(2,1)} %get-tuple-element.116), calls=%async_computation.6 | async-start | bytes 1048576 | tf_op jit(solution)/shard_map/all_to_all | solution.py:755
  191.2 1.7 collective-permute-done.27.refs_16_
  192.8 1.5 collective-permute-start.19
  194.3 1.5 collective-permute-start.18
  196.4 1.0 collective-permute-done.21.refs_1_
  197.9 1.0 collective-permute-done.23.refs_5_
  201.0 0.9 copy-done.11
  201.9 0.9 copy-done.13
  202.8 4.9 %shard_map.144 = (bf16[128,2176]{1,0:T(8,128)(2,1)S(1)}, bf16[128,2176]{1,0:T(8,128)(2,1)}) custom-call(s32[2]{0:T(128)S(1)} %copy-done.16, bf16[128,512]{1,0:T(8,128)(2,1)S(1)} %copy-done.7, bf16[128,512]{1,0:T(8,128)(2,1)S(1)} %collective-permute-done.21.refs_1_, bf16[128,512]{1,0:T(8,128)(2,1)S(1)} %copy-done.9, ...), custom_call_target="tpu_custom_call" | custom-call | flops 1073741824 | bytes 8388608 | tf_op jit(solution)/shard_map/pallas_call | solution.py:643
  207.7 2.8 %collective-permute-done.19.refs_12_ = bf16[128,2176]{1,0:T(8,128)(2,1)} collective-permute-done((bf16[128,2176]{1,0:T(8,128)(2,1)S(1)}, bf16[128,2176]{1,0:T(8,128)(2,1)}, u32[]{:S(2)}, u32[]{:S(2)}) %collective-permute-start.19) | collective-permute-done | bytes 557088 | tf_op jit(solution)/shard_map/ppermute | solution.py:752
  211.3 1.2 collective-permute-start.38
  213.2 5.5 %shard_map.146 = bf16[16,128,128]{2,1,0:T(8,128)(2,1)} custom-call(bf16[16,128,128]{2,1,0:T(8,128)(2,1)S(1)} %all-to-all-done.6.own_ref, bf16[16,128,128]{2,1,0:T(8,128)(2,1)S(1)} %collective-permute-done.31.other_ref, f8e4m3fn[2048,2048]{1,0:T(32,128)(4,1)} %shard_map.137.refs_0_, f8e4m3fn[2048,2048]{1,0:T(32,128)(4,1)} %shard_map.139.refs_1_), custom_call_target="tpu_custom_call" | custom-call | flops 2147483648 | bytes 8388608 | tf_op jit(solution)/shard_map/pallas_call | solution.py:297
  218.7 5.4 %all-to-all-start.7 = ((bf16[16,128,128]{2,1,0:T(8,128)(2,1)}), bf16[16,128,128]{2,1,0:T(8,128)(2,1)S(1)}, u32[]{:S(2)}, u32[]{:S(2)}) async-start(bf16[16,128,128]{2,1,0:T(8,128)(2,1)} %shard_map.146), calls=%async_computation.7 | async-start | bytes 1048576 | tf_op jit(solution)/shard_map/all_to_all | solution.py:755
  224.7 2.3 collective-permute-done.38.refs_14_
  227.5 1.3 collective-permute-done.32.refs_1_
  229.2 1.0 collective-permute-done.33.refs_3_
  230.7 1.0 collective-permute-done.34.refs_5_
  231.7 1.2 collective-permute-start.30
  237.2 5.0 %shard_map.148 = (bf16[64,2176]{1,0:T(8,128)(2,1)S(1)}, bf16[64,2176]{1,0:T(8,128)(2,1)}, bf16[64,2176]{1,0:T(8,128)(2,1)}, bf16[64,2176]{1,0:T(8,128)(2,1)}) custom-call(s32[2]{0:T(128)S(1)} %copy-done.17, bf16[128,512]{1,0:T(8,128)(2,1)S(1)} %copy-done.4, bf16[128,512]{1,0:T(8,128)(2,1)S(1)} %collective-permute-done.32.refs_1_, ...), custom_call_target="tpu_custom_call" | custom-call | flops 1073741824 | bytes 8388608 | tf_op jit(solution)/shard_map/pallas_call | solution.py:643
  242.2 1.2 collective-permute-start.40
  244.1 1.6 collective-permute-start.42
  246.4 1.1 shard_map.147
  249.0 7.7 %collective-permute-done.40.refs_1_ = bf16[64,2176]{1,0:T(8,128)(2,1)S(1)} collective-permute-done((bf16[64,2176]{1,0:T(8,128)(2,1)}, bf16[64,2176]{1,0:T(8,128)(2,1)S(1)}, u32[]{:S(2)}, u32[]{:S(2)}) %collective-permute-start.40) | collective-permute-done | bytes 278560 | tf_op jit(solution)/shard_map/ppermute | solution.py:778
  256.6 9.5 %collective-permute-done.41.refs_2_ = bf16[64,2176]{1,0:T(8,128)(2,1)S(1)} collective-permute-done((bf16[64,2176]{1,0:T(8,128)(2,1)}, bf16[64,2176]{1,0:T(8,128)(2,1)S(1)}, u32[]{:S(2)}, u32[]{:S(2)}) %collective-permute-start.41) | collective-permute-done | bytes 278560 | tf_op jit(solution)/shard_map/ppermute | solution.py:778
  266.1 7.2 %collective-permute-done.42.refs_3_ = bf16[64,2176]{1,0:T(8,128)(2,1)} collective-permute-done((bf16[64,2176]{1,0:T(8,128)(2,1)}, bf16[64,2176]{1,0:T(8,128)(2,1)}, u32[]{:S(2)}, u32[]{:S(2)}) %collective-permute-start.42) | collective-permute-done | bytes 278560 | tf_op jit(solution)/shard_map/ppermute | solution.py:778
  273.3 1.9 shard_map.150
  (133 shorter events, 21.5 us)
Async XLA Ops:
  1.7 13.3 %collective-permute-start.2 = (s32[32,256]{1,0:T(8,128)S(1)}, s32[32,256]{1,0:T(8,128)S(1)}, u32[]{:S(2)}, u32[]{:S(2)}) collective-permute-start(s32[32,256]{1,0:T(8,128)S(1)} %reshape.63), channel_id=1, source_target_pairs={{0,24},{8,16},{16,8},{24,0},{1,25},{9,17},{17,9},{25,1},{2,26},{10... | collective-permute-start | bytes 98312 | tf_op jit(solution)/shard_map/ppermute | solution.py:752
  4.2 10.8 %collective-permute-start.1 = (s32[32,256]{1,0:T(8,128)S(1)}, s32[32,256]{1,0:T(8,128)S(1)}, u32[]{:S(2)}, u32[]{:S(2)}) collective-permute-start(s32[32,256]{1,0:T(8,128)S(1)} %reshape.63), channel_id=1, source_target_pairs={{0,16},{8,24},{16,0},{24,8},{1,17},{9,25},{17,1},{25,9},{2,18},{10... | collective-permute-start | bytes 98312 | tf_op jit(solution)/shard_map/ppermute | solution.py:752
  4.7 10.3 %collective-permute-start = (s32[32,256]{1,0:T(8,128)S(1)}, s32[32,256]{1,0:T(8,128)S(1)}, u32[]{:S(2)}, u32[]{:S(2)}) collective-permute-start(s32[32,256]{1,0:T(8,128)S(1)} %reshape.63), channel_id=1, source_target_pairs={{0,8},{8,0},{16,24},{24,16},{1,9},{9,1},{17,25},{25,17},{2,10},{10... | collective-permute-start | bytes 98312 | tf_op jit(solution)/shard_map/ppermute | solution.py:752
  7.6 22.1 %all-to-all-start = ((bf16[16,128,128]{2,1,0:T(8,128)(2,1)}), bf16[16,128,128]{2,1,0:T(8,128)(2,1)S(1)}, u32[]{:S(2)}, u32[]{:S(2)}) async-start(bf16[16,128,128]{2,1,0:T(8,128)(2,1)} %bitcast.3), calls=%async_computation | async-start | bytes 1048576 | tf_op jit(solution)/shard_map/all_to_all | solution.py:755
  14.9 57.2 %copy-start.15 = (s32[2]{0:T(128)}, s32[2]{0:T(128)S(1)}, u32[]{:S(2)}) copy-start(s32[2]{0:T(128)S(1)} %pad_add_fusion.1.place_ref.at_ref) | copy-start | bytes 28
  29.6 14.6 %copy-start.32 = (s32[128]{0:T(128)S(1)}, s32[128]{0:T(128)}, u32[]{:S(2)}) copy-start(s32[128]{0:T(128)} %param.15) | copy-start | bytes 1540
  29.6 1.9 collective-permute-start.3
  37.4 20.4 %all-to-all-start.1 = ((bf16[16,128,128]{2,1,0:T(8,128)(2,1)}), bf16[16,128,128]{2,1,0:T(8,128)(2,1)S(1)}, u32[]{:S(2)}, u32[]{:S(2)}) async-start(bf16[16,128,128]{2,1,0:T(8,128)(2,1)} %shard_map.136), calls=%async_computation.1 | async-start | bytes 1048576 | tf_op jit(solution)/shard_map/all_to_all | solution.py:755
  44.4 13.4 %copy-start.1 = (f32[128,1]{1,0:T(8,128)}, f32[128,1]{1,0:T(8,128)S(1)}, u32[]{:S(2)}) copy-start(f32[128,1]{1,0:T(8,128)S(1)} %copy.23.valid_ref) | copy-start | bytes 1540
  64.2 18.9 %copy-start.20 = (f32[8,128]{1,0:T(8,128)}, f32[8,128]{1,0:T(8,128)S(1)}, u32[]{:S(2)}) copy-start(f32[8,128]{1,0:T(8,128)S(1)} %get-tuple-element.94.stat_ref) | copy-start | bytes 12292
  64.2 162.8 %copy-start.3 = (bf16[128,512]{1,0:T(8,128)(2,1)}, bf16[128,512]{1,0:T(8,128)(2,1)S(1)}, u32[]{:S(2)}) copy-start(bf16[128,512]{1,0:T(8,128)(2,1)S(1)} %get-tuple-element.138.refs_0_) | copy-start | bytes 393220
  64.2 19.3 %all-to-all-start.2 = ((bf16[16,128,128]{2,1,0:T(8,128)(2,1)}), bf16[16,128,128]{2,1,0:T(8,128)(2,1)S(1)}, u32[]{:S(2)}, u32[]{:S(2)}) async-start(bf16[16,128,128]{2,1,0:T(8,128)(2,1)} %get-tuple-element.87), calls=%async_computation.2 | async-start | bytes 1048576 | tf_op jit(solution)/shard_map/all_to_all | solution.py:755
  70.7 1.4 collective-permute-start.4
  83.5 1.9 collective-permute-start.5
  91.2 21.2 %all-to-all-start.3 = ((bf16[16,128,128]{2,1,0:T(8,128)(2,1)}), bf16[16,128,128]{2,1,0:T(8,128)(2,1)S(1)}, u32[]{:S(2)}, u32[]{:S(2)}) async-start(bf16[16,128,128]{2,1,0:T(8,128)(2,1)} %shard_map.140), calls=%async_computation.3 | async-start | bytes 1048576 | tf_op jit(solution)/shard_map/all_to_all | solution.py:755
  98.5 8.8 %collective-permute-start.6 = (bf16[128,512]{1,0:T(8,128)(2,1)S(1)}, bf16[128,512]{1,0:T(8,128)(2,1)S(1)}, u32[]{:S(2)}, u32[]{:S(2)}) collective-permute-start(bf16[128,512]{1,0:T(8,128)(2,1)S(1)} %get-tuple-element.90), channel_id=1, source_target_pairs={{0,8},{8,0},{16,24},{24,16},{1,9},{9,1},{17,25},{25,17},{2,10},{10... | collective-permute-start | bytes 393224 | tf_op jit(solution)/shard_map/ppermute | solution.py:752
  99.9 9.5 %collective-permute-start.7 = (bf16[128,512]{1,0:T(8,128)(2,1)S(1)}, bf16[128,512]{1,0:T(8,128)(2,1)}, u32[]{:S(2)}, u32[]{:S(2)}) collective-permute-start(bf16[128,512]{1,0:T(8,128)(2,1)S(1)} %get-tuple-element.91), channel_id=1, source_target_pairs={{0,16},{8,24},{16,0},{24,8},{1,17},{9,25},{17,1},{25,9},{2,18},{10... | collective-permute-start | bytes 393224 | tf_op jit(solution)/shard_map/ppermute | solution.py:752
  101.4 11.0 %collective-permute-start.8 = (bf16[128,512]{1,0:T(8,128)(2,1)S(1)}, bf16[128,512]{1,0:T(8,128)(2,1)}, u32[]{:S(2)}, u32[]{:S(2)}) collective-permute-start(bf16[128,512]{1,0:T(8,128)(2,1)S(1)} %get-tuple-element.92), channel_id=1, source_target_pairs={{0,24},{8,16},{16,8},{24,0},{1,25},{9,17},{17,9},{25,1},{2,26},{10... | collective-permute-start | bytes 393224 | tf_op jit(solution)/shard_map/ppermute | solution.py:752
  107.3 121.5 %copy-start.5 = (bf16[128,512]{1,0:T(8,128)(2,1)}, bf16[128,512]{1,0:T(8,128)(2,1)S(1)}, u32[]{:S(2)}) copy-start(bf16[128,512]{1,0:T(8,128)(2,1)S(1)} %collective-permute-done.6.refs_2_) | copy-start | bytes 393220
  122.3 55.0 %copy-start.2 = (bf16[16,128,128]{2,1,0:T(8,128)(2,1)S(1)}, bf16[16,128,128]{2,1,0:T(8,128)(2,1)}, u32[]{:S(2)}) copy-start(bf16[16,128,128]{2,1,0:T(8,128)(2,1)} %get-tuple-element.115.extra_ref) | copy-start | bytes 1572868
  122.3 55.0 %copy-start.18 = (f32[1,128]{1,0:T(1,128)S(1)}, f32[1,128]{1,0:T(1,128)}, u32[]{:S(2)}) copy-start(f32[1,128]{1,0:T(1,128)} %divide_bitcast_fusion.inverse_ref) | copy-start | bytes 1540
  122.3 25.8 %all-to-all-start.4 = ((bf16[16,128,128]{2,1,0:T(8,128)(2,1)}), bf16[16,128,128]{2,1,0:T(8,128)(2,1)S(1)}, u32[]{:S(2)}, u32[]{:S(2)}) async-start(bf16[16,128,128]{2,1,0:T(8,128)(2,1)} %get-tuple-element.97), calls=%async_computation.4 | async-start | bytes 1048576 | tf_op jit(solution)/shard_map/all_to_all | solution.py:755
  128.0 3.1 %collective-permute-start.11 = (bf16[128,2176]{1,0:T(8,128)(2,1)}, bf16[128,2176]{1,0:T(8,128)(2,1)S(1)}, u32[]{:S(2)}, u32[]{:S(2)}) collective-permute-start(bf16[128,2176]{1,0:T(8,128)(2,1)} %get-tuple-element.98.refs_8_), channel_id=1, source_target_pairs={{0,4},{4,0},{1,5},{5,1},{2,6},{6,2},{3,7},{7,3},{8,12},{12,8},{9,1... | collective-permute-start | bytes 1671176 | tf_op jit(solution)/shard_map/ppermute | solution.py:749
  128.0 20.1 %collective-permute-start.10 = (bf16[128,2176]{1,0:T(8,128)(2,1)}, bf16[128,2176]{1,0:T(8,128)(2,1)S(1)}, u32[]{:S(2)}, u32[]{:S(2)}) collective-permute-start(bf16[128,2176]{1,0:T(8,128)(2,1)} %get-tuple-element.98.refs_8_), channel_id=1, source_target_pairs={{0,16},{8,24},{16,0},{24,8},{1,17},{9,25},{17,1},{25,9},{2,18},{10... | collective-permute-start | bytes 1671176 | tf_op jit(solution)/shard_map/ppermute | solution.py:752
  129.6 18.5 %collective-permute-start.9 = (bf16[128,2176]{1,0:T(8,128)(2,1)}, bf16[128,2176]{1,0:T(8,128)(2,1)S(1)}, u32[]{:S(2)}, u32[]{:S(2)}) collective-permute-start(bf16[128,2176]{1,0:T(8,128)(2,1)} %get-tuple-element.98.refs_8_), channel_id=1, source_target_pairs={{0,8},{8,0},{16,24},{24,16},{1,9},{9,1},{17,25},{25,17},{2,10},{10... | collective-permute-start | bytes 1671176 | tf_op jit(solution)/shard_map/ppermute | solution.py:752
  131.1 17.2 %copy-start.25 = (bf16[128,2176]{1,0:T(8,128)(2,1)}, bf16[128,2176]{1,0:T(8,128)(2,1)S(1)}, u32[]{:S(2)}) copy-start(bf16[128,2176]{1,0:T(8,128)(2,1)S(1)} %collective-permute-done.11.refs_9_) | copy-start | bytes 1671172
  148.1 29.2 %copy-start.22 = (bf16[128,2176]{1,0:T(8,128)(2,1)}, bf16[128,2176]{1,0:T(8,128)(2,1)S(1)}, u32[]{:S(2)}) copy-start(bf16[128,2176]{1,0:T(8,128)(2,1)S(1)} %collective-permute-done.10.refs_12_) | copy-start | bytes 1671172
  148.1 29.2 %copy-start.23 = (bf16[128,2176]{1,0:T(8,128)(2,1)}, bf16[128,2176]{1,0:T(8,128)(2,1)S(1)}, u32[]{:S(2)}) copy-start(bf16[128,2176]{1,0:T(8,128)(2,1)S(1)} %collective-permute-done.9.refs_10_) | copy-start | bytes 1671172
  148.1 2.2 collective-permute-start.12
  148.3 18.5 %copy-start.31 = (bf16[128,512]{1,0:T(8,128)(2,1)S(1)}, bf16[128,512]{1,0:T(8,128)(2,1)}, u32[]{:S(2)}) copy-start(bf16[128,512]{1,0:T(8,128)(2,1)} %get-tuple-element.113) | copy-start | bytes 393220
  148.3 9.1 %collective-permute-start.14 = (bf16[64,2176]{1,0:T(8,128)(2,1)S(1)}, bf16[64,2176]{1,0:T(8,128)(2,1)S(1)}, u32[]{:S(2)}, u32[]{:S(2)}) collective-permute-start(bf16[64,2176]{1,0:T(8,128)(2,1)S(1)} %slice.7), channel_id=1, source_target_pairs={{0,8},{8,0},{16,24},{24,16},{1,9},{9,1},{17,25},{25,17},{2,10},{10... | collective-permute-start | bytes 835592 | tf_op jit(solution)/shard_map/ppermute | solution.py:752
  149.9 8.8 %collective-permute-start.13 = (bf16[64,2176]{1,0:T(8,128)(2,1)S(1)}, bf16[64,2176]{1,0:T(8,128)(2,1)S(1)}, u32[]{:S(2)}, u32[]{:S(2)}) collective-permute-start(bf16[64,2176]{1,0:T(8,128)(2,1)S(1)} %slice.6), channel_id=1, source_target_pairs={{0,16},{8,24},{16,0},{24,8},{1,17},{9,25},{17,1},{25,9},{2,18},{10... | collective-permute-start | bytes 835592 | tf_op jit(solution)/shard_map/ppermute | solution.py:752
  155.9 43.2 %copy-start.16 = (s32[2]{0:T(128)S(1)}, s32[2]{0:T(128)}, u32[]{:S(2)}) copy-start(s32[2]{0:T(128)} %copy-done.15) | copy-start | bytes 28
  158.6 18.7 %all-to-all-start.5 = ((bf16[16,128,128]{2,1,0:T(8,128)(2,1)}), bf16[16,128,128]{2,1,0:T(8,128)(2,1)S(1)}, u32[]{:S(2)}, u32[]{:S(2)}) async-start(bf16[16,128,128]{2,1,0:T(8,128)(2,1)} %shard_map.142), calls=%async_computation.5 | async-start | bytes 1048576 | tf_op jit(solution)/shard_map/all_to_all | solution.py:755
  163.8 10.1 %collective-permute-start.15 = (bf16[128,512]{1,0:T(8,128)(2,1)}, bf16[128,512]{1,0:T(8,128)(2,1)S(1)}, u32[]{:S(2)}, u32[]{:S(2)}) collective-permute-start(bf16[128,512]{1,0:T(8,128)(2,1)} %get-tuple-element.111), channel_id=1, source_target_pairs={{0,8},{8,0},{16,24},{24,16},{1,9},{9,1},{17,25},{25,17},{2,10},{10... | collective-permute-start | bytes 393224 | tf_op jit(solution)/shard_map/ppermute | solution.py:752
  165.3 10.4 %collective-permute-start.16 = (bf16[128,512]{1,0:T(8,128)(2,1)}, bf16[128,512]{1,0:T(8,128)(2,1)S(1)}, u32[]{:S(2)}, u32[]{:S(2)}) collective-permute-start(bf16[128,512]{1,0:T(8,128)(2,1)} %get-tuple-element.112), channel_id=1, source_target_pairs={{0,16},{8,24},{16,0},{24,8},{1,17},{9,25},{17,1},{25,9},{2,18},{10... | collective-permute-start | bytes 393224 | tf_op jit(solution)/shard_map/ppermute | solution.py:752
  166.8 10.5 %collective-permute-start.17 = (bf16[128,512]{1,0:T(8,128)(2,1)S(1)}, bf16[128,512]{1,0:T(8,128)(2,1)S(1)}, u32[]{:S(2)}, u32[]{:S(2)}) collective-permute-start(bf16[128,512]{1,0:T(8,128)(2,1)S(1)} %copy-done.31), channel_id=1, source_target_pairs={{0,24},{8,16},{16,8},{24,0},{1,25},{9,17},{17,9},{25,1},{2,26},{10... | collective-permute-start | bytes 393224 | tf_op jit(solution)/shard_map/ppermute | solution.py:752
  184.4 26.9 %all-to-all-start.6 = ((bf16[16,128,128]{2,1,0:T(8,128)(2,1)}), bf16[16,128,128]{2,1,0:T(8,128)(2,1)S(1)}, u32[]{:S(2)}, u32[]{:S(2)}) async-start(bf16[16,128,128]{2,1,0:T(8,128)(2,1)} %get-tuple-element.116), calls=%async_computation.6 | async-start | bytes 1048576 | tf_op jit(solution)/shard_map/all_to_all | solution.py:755
  190.1 5.8 %collective-permute-start.25 = (bf16[128,2176]{1,0:T(8,128)(2,1)}, bf16[128,2176]{1,0:T(8,128)(2,1)S(1)}, u32[]{:S(2)}, u32[]{:S(2)}) collective-permute-start(bf16[128,2176]{1,0:T(8,128)(2,1)} %copy-done.23), channel_id=1, source_target_pairs={{0,4},{4,0},{1,5},{5,1},{2,6},{6,2},{3,7},{7,3},{8,12},{12,8},{9,1... | collective-permute-start | bytes 1671176 | tf_op jit(solution)/shard_map/ppermute | solution.py:749
  190.1 5.8 %collective-permute-start.26 = (bf16[128,2176]{1,0:T(8,128)(2,1)}, bf16[128,2176]{1,0:T(8,128)(2,1)S(1)}, u32[]{:S(2)}, u32[]{:S(2)}) collective-permute-start(bf16[128,2176]{1,0:T(8,128)(2,1)} %copy-done.22), channel_id=1, source_target_pairs={{0,4},{4,0},{1,5},{5,1},{2,6},{6,2},{3,7},{7,3},{8,12},{12,8},{9,1... | collective-permute-start | bytes 1671176 | tf_op jit(solution)/shard_map/ppermute | solution.py:749
  190.6 2.2 collective-permute-start.27
  190.7 3.7 %collective-permute-start.28 = (bf16[64,2176]{1,0:T(8,128)(2,1)S(1)}, bf16[64,2176]{1,0:T(8,128)(2,1)S(1)}, u32[]{:S(2)}, u32[]{:S(2)}) collective-permute-start(bf16[64,2176]{1,0:T(8,128)(2,1)S(1)} %collective-permute-done.14.refs_15_), channel_id=1, source_target_pairs={{0,4},{4,0},{1,5},{5,1},{2,6},{6,2},{3,7},{7,3},{8,12},{12,8},{9,1... | collective-permute-start | bytes 835592 | tf_op jit(solution)/shard_map/ppermute | solution.py:749
  191.1 16.6 %collective-permute-start.20 = (bf16[128,2176]{1,0:T(8,128)(2,1)S(1)}, bf16[128,2176]{1,0:T(8,128)(2,1)S(1)}, u32[]{:S(2)}, u32[]{:S(2)}) collective-permute-start(bf16[128,2176]{1,0:T(8,128)(2,1)S(1)} %get-tuple-element.142.refs_8_), channel_id=1, source_target_pairs={{0,4},{4,0},{1,5},{5,1},{2,6},{6,2},{3,7},{7,3},{8,12},{12,8},{9,1... | collective-permute-start | bytes 1671176 | tf_op jit(solution)/shard_map/ppermute | solution.py:749
  192.8 17.7 %collective-permute-start.19 = (bf16[128,2176]{1,0:T(8,128)(2,1)S(1)}, bf16[128,2176]{1,0:T(8,128)(2,1)}, u32[]{:S(2)}, u32[]{:S(2)}) collective-permute-start(bf16[128,2176]{1,0:T(8,128)(2,1)S(1)} %get-tuple-element.142.refs_8_), channel_id=1, source_target_pairs={{0,16},{8,24},{16,0},{24,8},{1,17},{9,25},{17,1},{25,9},{2,18},{10... | collective-permute-start | bytes 1671176 | tf_op jit(solution)/shard_map/ppermute | solution.py:752
  194.3 17.0 %collective-permute-start.18 = (bf16[128,2176]{1,0:T(8,128)(2,1)S(1)}, bf16[128,2176]{1,0:T(8,128)(2,1)}, u32[]{:S(2)}, u32[]{:S(2)}) collective-permute-start(bf16[128,2176]{1,0:T(8,128)(2,1)S(1)} %get-tuple-element.142.refs_8_), channel_id=1, source_target_pairs={{0,8},{8,0},{16,24},{24,16},{1,9},{9,1},{17,25},{25,17},{2,10},{10... | collective-permute-start | bytes 1671176 | tf_op jit(solution)/shard_map/ppermute | solution.py:752
  195.8 1.6 collective-permute-start.21
  195.9 1.7 collective-permute-start.22
  197.4 1.6 collective-permute-start.23
  197.6 1.6 collective-permute-start.24
  211.3 1.9 collective-permute-start.31
  211.3 15.7 %collective-permute-start.38 = (bf16[128,2176]{1,0:T(8,128)(2,1)}, bf16[128,2176]{1,0:T(8,128)(2,1)}, u32[]{:S(2)}, u32[]{:S(2)}) collective-permute-start(bf16[128,2176]{1,0:T(8,128)(2,1)} %collective-permute-done.18.refs_10_), channel_id=1, source_target_pairs={{0,16},{8,24},{16,0},{24,8},{1,17},{9,25},{17,1},{25,9},{2,18},{10... | collective-permute-start | bytes 1671176 | tf_op jit(solution)/shard_map/ppermute | solution.py:752
  212.5 18.0 %collective-permute-start.29 = (bf16[128,2176]{1,0:T(8,128)(2,1)}, bf16[128,2176]{1,0:T(8,128)(2,1)S(1)}, u32[]{:S(2)}, u32[]{:S(2)}) collective-permute-start(bf16[128,2176]{1,0:T(8,128)(2,1)} %get-tuple-element.130), channel_id=1, source_target_pairs={{0,1},{1,0},{2,3},{3,2},{4,5},{5,4},{6,7},{7,6},{8,9},{9,8},{10,11... | collective-permute-start | bytes 1671176 | tf_op jit(solution)/shard_map/ppermute | solution.py:778
  218.7 27.0 %all-to-all-start.7 = ((bf16[16,128,128]{2,1,0:T(8,128)(2,1)}), bf16[16,128,128]{2,1,0:T(8,128)(2,1)S(1)}, u32[]{:S(2)}, u32[]{:S(2)}) async-start(bf16[16,128,128]{2,1,0:T(8,128)(2,1)} %shard_map.146), calls=%async_computation.7 | async-start | bytes 1048576 | tf_op jit(solution)/shard_map/all_to_all | solution.py:755
  224.1 8.7 %collective-permute-start.36 = (bf16[128,2176]{1,0:T(8,128)(2,1)}, bf16[128,2176]{1,0:T(8,128)(2,1)S(1)}, u32[]{:S(2)}, u32[]{:S(2)}) collective-permute-start(bf16[128,2176]{1,0:T(8,128)(2,1)} %collective-permute-done.18.refs_10_), channel_id=1, source_target_pairs={{0,4},{4,0},{1,5},{5,1},{2,6},{6,2},{3,7},{7,3},{8,12},{12,8},{9,1... | collective-permute-start | bytes 1671176 | tf_op jit(solution)/shard_map/ppermute | solution.py:749
  224.2 8.7 %collective-permute-start.37 = (bf16[128,2176]{1,0:T(8,128)(2,1)}, bf16[128,2176]{1,0:T(8,128)(2,1)S(1)}, u32[]{:S(2)}, u32[]{:S(2)}) collective-permute-start(bf16[128,2176]{1,0:T(8,128)(2,1)} %collective-permute-done.19.refs_12_), channel_id=1, source_target_pairs={{0,4},{4,0},{1,5},{5,1},{2,6},{6,2},{3,7},{7,3},{8,12},{12,8},{9,1... | collective-permute-start | bytes 1671176 | tf_op jit(solution)/shard_map/ppermute | solution.py:749
  227.0 5.9 %collective-permute-start.39 = (bf16[128,2176]{1,0:T(8,128)(2,1)}, bf16[128,2176]{1,0:T(8,128)(2,1)S(1)}, u32[]{:S(2)}, u32[]{:S(2)}) collective-permute-start(bf16[128,2176]{1,0:T(8,128)(2,1)} %collective-permute-done.38.refs_14_), channel_id=1, source_target_pairs={{0,4},{4,0},{1,5},{5,1},{2,6},{6,2},{3,7},{7,3},{8,12},{12,8},{9,1... | collective-permute-start | bytes 1671176 | tf_op jit(solution)/shard_map/ppermute | solution.py:749
  227.0 1.8 collective-permute-start.32
  228.8 1.4 collective-permute-start.33
  230.1 1.6 collective-permute-start.34
  230.5 2.3 collective-permute-start.35
  231.7 16.4 %collective-permute-start.30 = (bf16[64,2176]{1,0:T(8,128)(2,1)S(1)}, bf16[64,2176]{1,0:T(8,128)(2,1)S(1)}, u32[]{:S(2)}, u32[]{:S(2)}) collective-permute-start(bf16[64,2176]{1,0:T(8,128)(2,1)S(1)} %shard_map.145), channel_id=1, source_target_pairs={{0,2},{1,3},{2,0},{3,1},{4,6},{5,7},{6,4},{7,5},{8,10},{9,11},{10,... | collective-permute-start | bytes 835592 | tf_op jit(solution)/shard_map/ppermute | solution.py:778
  242.2 14.4 %collective-permute-start.40 = (bf16[64,2176]{1,0:T(8,128)(2,1)}, bf16[64,2176]{1,0:T(8,128)(2,1)S(1)}, u32[]{:S(2)}, u32[]{:S(2)}) collective-permute-start(bf16[64,2176]{1,0:T(8,128)(2,1)} %get-tuple-element.147), channel_id=1, source_target_pairs={{0,1},{1,0},{2,3},{3,2},{4,5},{5,4},{6,7},{7,6},{8,9},{9,8},{10,11... | collective-permute-start | bytes 835592 | tf_op jit(solution)/shard_map/ppermute | solution.py:778
  243.4 22.7 %collective-permute-start.41 = (bf16[64,2176]{1,0:T(8,128)(2,1)}, bf16[64,2176]{1,0:T(8,128)(2,1)S(1)}, u32[]{:S(2)}, u32[]{:S(2)}) collective-permute-start(bf16[64,2176]{1,0:T(8,128)(2,1)} %get-tuple-element.148), channel_id=1, source_target_pairs={{0,2},{1,3},{2,0},{3,1},{4,6},{5,7},{6,4},{7,5},{8,10},{9,11},{10,... | collective-permute-start | bytes 835592 | tf_op jit(solution)/shard_map/ppermute | solution.py:778
  244.1 29.2 %collective-permute-start.42 = (bf16[64,2176]{1,0:T(8,128)(2,1)}, bf16[64,2176]{1,0:T(8,128)(2,1)}, u32[]{:S(2)}, u32[]{:S(2)}) collective-permute-start(bf16[64,2176]{1,0:T(8,128)(2,1)} %get-tuple-element.149), channel_id=1, source_target_pairs={{0,3},{1,2},{2,1},{3,0},{4,7},{5,6},{6,5},{7,4},{8,11},{9,10},{10,... | collective-permute-start | bytes 835592 | tf_op jit(solution)/shard_map/ppermute | solution.py:778
  (20 other events, 72.5 us)
